TPU v7x, 768 devices: a whole 4x8x12 slice. The times are simulated.
768 devices in a mesh: dp: 128 (over y, z_lo, x), tensor: 6 (over z_hi, core).
Axes of the slice: x: 4, y: 8, z: 12 (z_hi: 3, z_lo: 4; z = z_hi * 4 + z_lo), core: 2. Of those that a mesh axis runs over, the one named last changes fastest.
Arguments:
- table_sums: bfloat16 [512, 256, 192], P(None, 'dp', 'tensor'), may hold values from -6 to 6
- bag_lengths: int32 [512, 256], P(None, 'dp'), may hold values from 1 to 8
- feature_slot: int32 [256], replicated, may hold values from 0 to 255, each once
- fm_project: bfloat16 [256, 8], replicated, may hold values from -0.375 to 0.375
- ln_gain: float32 [2048], replicated, may hold values from 0.25 to 1.75
- up_weight: bfloat16 [2048, 6144], P(None, 'tensor'), may hold values from -0.125 to 0.125
- out_weight: bfloat16 [6144, 1536], P('tensor'), may hold values from -0.078125 to 0.078125
- lc_weight: bfloat16 [256, 8], replicated, may hold values from -0.375 to 0.375
- cotangent: bfloat16 [512, 16, 192], P('dp'), may hold values from -6 to 6
Outputs:
- layer_out: bfloat16 [512, 16, 192], P('dp', None, 'tensor')
- grad_sums: bfloat16 [512, 256, 192], P(None, 'dp', 'tensor')
Inputs may be any that keep to these rules, and one draw needn't show every extreme that they name: `feature_slot`: each slot number appears once.
All inputs are finite; a program needn't handle non-finite values.
Results may differ from a plain program's by a relative error of at most 0.011.
Values may be sent and summed in bfloat16 or wider, within the bound.
No kernel may reach another device: no remote copies, remote signals or barrier semaphores. Data moves between devices by JAX's collectives and lax.ppermute only.
A program may use at most 64 MiB of HBM per device.

v0:
```python
import jax
import jax.numpy as jnp
from jax import lax
from jax.sharding import PartitionSpec as P

D = 192
NF = 8


exact_precision = lax.Precision.HIGHEST


def slot_inverse(feature_slot):
    slot_count = feature_slot.shape[0]
    positions = jnp.arange(slot_count, dtype=jnp.int32)
    matches = feature_slot[:, None] == positions[None, :]
    return jnp.sum(jnp.where(matches, positions[:, None], 0), axis=0)


def shards(
    table_sums,
    bag_lengths,
    feature_slot,
    fm_project,
    ln_gain,
    up_weight,
    out_weight,
    lc_weight,
    cotangent,
):
    slice_width = table_sums.shape[2]
    lengths = bag_lengths.astype(jnp.float32)[:, :, None]
    pooled = (table_sums.astype(jnp.float32) / lengths).astype(jnp.bfloat16)
    arrived = lax.all_to_all(pooled, "dp", split_axis=0, concat_axis=1, tiled=True)
    embedded_features = jnp.take(arrived, feature_slot, axis=1).astype(jnp.float32)
    sample_count = embedded_features.shape[0]
    projection_weight = fm_project.astype(jnp.float32)
    mixing_weight = lc_weight.astype(jnp.float32)
    slot_coupling_matrix = jnp.einsum(
        "sfd,fk->sdk", embedded_features, projection_weight, precision=exact_precision
    )
    gram_local = jnp.einsum(
        "sfd,sdk->sfk", embedded_features, slot_coupling_matrix, precision=exact_precision
    )
    gram_block = lax.psum(gram_local, "tensor")
    flattened = gram_block.reshape(sample_count, -1)
    centered = flattened - jnp.mean(flattened, axis=1, keepdims=True)
    scale_inv = lax.rsqrt(jnp.mean(centered * centered, axis=1, keepdims=True) + 1e-05)
    whitened = centered * scale_inv
    normed = (whitened * ln_gain).astype(jnp.bfloat16)
    up_proj = jnp.dot(normed, up_weight, preferred_element_type=jnp.float32)
    sigmoid_up = jax.nn.sigmoid(up_proj)
    hidden = (up_proj * sigmoid_up).astype(jnp.bfloat16)
    partial_out = jnp.dot(hidden, out_weight, preferred_element_type=jnp.float32).reshape(
        sample_count, NF, D
    )
    offset = lax.axis_index("tensor") * slice_width
    summed = lax.psum(partial_out, "tensor")
    fm_out = lax.dynamic_slice_in_dim(summed, offset, slice_width, 2)
    linear_component = jnp.einsum(
        "gnh,nx->gxh", embedded_features, mixing_weight, precision=exact_precision
    )
    layer_out = jnp.concatenate([fm_out, linear_component], axis=1).astype(jnp.bfloat16)
    cot_fm = cotangent[:, :NF].reshape(sample_count, NF * D)
    d_hidden = jnp.dot(cot_fm, out_weight.T, preferred_element_type=jnp.float32)
    d_up = (d_hidden * (sigmoid_up + up_proj * sigmoid_up * (1.0 - sigmoid_up))).astype(
        jnp.bfloat16
    )
    d_norm = lax.psum(
        jnp.dot(d_up, up_weight.T, preferred_element_type=jnp.float32).astype(jnp.bfloat16),
        "tensor",
    ).astype(jnp.float32)
    grad_block = d_norm * ln_gain
    d_flat = scale_inv * (
        grad_block
        - jnp.mean(grad_block, axis=1, keepdims=True)
        - whitened * jnp.mean(grad_block * whitened, axis=1, keepdims=True)
    )
    gram_gradient = d_flat.reshape(gram_block.shape)
    coupling_gradient = jnp.einsum(
        "sfd,sfk->sdk", embedded_features, gram_gradient, precision=exact_precision
    )
    linear_cotangent_term = lax.dynamic_slice_in_dim(
        cotangent[:, NF:], offset, slice_width, 2
    ).astype(jnp.float32)
    inverse = slot_inverse(feature_slot)
    embedding_gradient = (
        jnp.einsum("tpx,tjx->tpj", gram_gradient, slot_coupling_matrix, precision=exact_precision)
        + jnp.einsum("zc,jtc->jzt", projection_weight, coupling_gradient, precision=exact_precision)
        + jnp.einsum("ka,waz->wkz", mixing_weight, linear_cotangent_term, precision=exact_precision)
    )
    d_slots = jnp.take(embedding_gradient, inverse, axis=1).astype(jnp.bfloat16)
    d_pooled = lax.all_to_all(d_slots, "dp", split_axis=1, concat_axis=0, tiled=True)
    grad_sums = (d_pooled.astype(jnp.float32) / lengths).astype(jnp.bfloat16)
    return (layer_out, grad_sums)


def solution(mesh):
    return jax.shard_map(
        shards,
        mesh=mesh,
        in_specs=(
            P(None, "dp", "tensor"),
            P(None, "dp"),
            P(),
            P(),
            P(),
            P(None, "tensor"),
            P("tensor", None),
            P(),
            P("dp", None, None),
        ),
        out_specs=(P("dp", None, "tensor"), P(None, "dp", "tensor")),
        check_vma=False,
    )
```

profile of v0, /device:TPU:1, one launch (start us, length us, event | category | flops | bytes accessed | tf_op | source)
XLA Modules:
  0.0 168.6 jit_solution(16662221852231209911)
XLA Ops:
  0.6 0.0 copy-start
  0.6 0.0 copy-start.3
  0.7 0.0 copy-start.4
  0.7 0.0 copy-start.2
  0.7 0.8 convert_element_type.48
  1.5 1.0 divide_convert_fusion.1
  2.5 0.2 copy.73
  2.7 0.8 reshape.96
  3.5 17.8 %all-to-all-start = ((bf16[128,2,128]{2,1,0:T(2,128)(2,1)}), bf16[128,2,128]{2,1,0:T(2,128)(2,1)S(1)}, u32[]{:S(2)}, u32[]{:S(2)}) async-start(bf16[128,2,128]{2,1,0:T(2,128)(2,1)} %reshape.96), calls=%async_computation | async-start | bytes 131072 | tf_op jit(solution)/shard_map/all_to_all | solution.py:34
  21.3 0.7 compare_and_fusion.1
  21.9 0.8 select_reduce_fusion
  22.7 0.7 compare_select_fusion.2
  23.4 0.7 fusion.25
  24.2 0.1 reshape.73
  24.3 1.6 convolution_bitcast_fusion
  25.9 6.0 %all-to-all-done = bf16[128,2,128]{2,1,0:T(2,128)(2,1)S(1)} async-done(((bf16[128,2,128]{2,1,0:T(2,128)(2,1)}), bf16[128,2,128]{2,1,0:T(2,128)(2,1)S(1)}, u32[]{:S(2)}, u32[]{:S(2)}) %all-to-all-start) | async-done | bytes 65568 | tf_op jit(solution)/shard_map/all_to_all | solution.py:34
  31.9 0.2 reshape.97
  32.1 0.3 copy.75
  32.4 0.2 copy.76
  32.6 1.7 gather_fusion
  34.3 1.3 select_bitcast_fusion
  35.6 0.1 copy.78
  35.7 0.0 copy-done.3
  35.7 0.1 fusion.2
  35.9 0.0 copy-done.4
  35.9 0.2 fusion.21
  36.0 0.2 fusion.27
  36.2 36.7 %psum.21 = f32[4,256,8]{1,2,0:T(8,128)S(1)} all-reduce(f32[4,256,8]{1,2,0:T(8,128)S(1)} %fusion.27), channel_id=1, replica_groups=mesh['dp'=128,'tensor'=6] {'tensor'}, use_global_device_ids=true, to_apply=%region_0.1 | all-reduce | flops 8192 | bytes 65536 | tf_op jit(solution)/shard_map/psum | solution.py:45
  72.9 1.0 copy.79
  73.9 0.1 reduce_sum.47
  74.0 0.2 multiply_reduce_fusion.1
  74.2 1.3 reshape.71
  75.5 0.0 copy-done.2
  75.5 2.9 %fusion.5 = f32[4,1024]{1,0:T(4,128)S(1)} fusion(bf16[2048,1024]{1,0:T(8,128)(2,1)} %param.14, f32[4,2048]{1,0:T(4,128)S(1)} %reshape.71, f32[2048]{0:T(1024)S(1)} %copy-done.2, f32[4]{0:T(128)S(1)} %add_rsqrt_fusion, f32[4]{0:T(128)S(1)} %broadcast_multiply_fusion.2), kind=kOutput, calls=%fused_computation.25 | convolution fusion | flops 16809984 | bytes 4251680 | tf_op jit(solution)/shard_map/dot_general | solution.py:51
  78.4 0.0 copy-done
  78.4 0.5 fusion.13
  78.9 0.0 copy-start.1
  78.9 4.2 %convolution_convert_fusion = bf16[4,2048]{1,0:T(4,128)(2,1)S(1)} fusion(bf16[2048,1024]{1,0:T(8,128)(2,1)} %param.14, bf16[4,1536]{1,0:T(4,128)(2,1)S(1)} %reshape.73, bf16[1024,1536]{1,0:T(8,128)(2,1)S(1)} %copy-done, f32[4,1024]{1,0:T(4,128)S(1)} %fusion.5), kind=kOutput, calls=%fused_computation.2 | convolution fusion | flops 29405184 | bytes 7385088 | tf_op jit(solution)/shard_map/dot_general | solution.py:70
  83.1 21.8 %psum.23 = bf16[4,2048]{1,0:T(4,128)(2,1)S(1)} all-reduce(bf16[4,2048]{1,0:T(4,128)(2,1)S(1)} %convolution_convert_fusion), channel_id=1, replica_groups=mesh['dp'=128,'tensor'=6] {'tensor'}, use_global_device_ids=true, to_apply=%region_5.6 | all-reduce | flops 8192 | bytes 32768 | tf_op jit(solution)/shard_map/psum | solution.py:69
  104.9 0.2 fusion.4
  105.1 0.1 reshape.72
  105.2 32.2 %psum.22 = bf16[4,8,192]{2,1,0:T(8,128)(2,1)S(1)} all-reduce(f32[4,8,192]{2,1,0:T(8,128)S(1)} %reshape.72), channel_id=1, replica_groups=mesh['dp'=128,'tensor'=6] {'tensor'}, use_global_device_ids=true, to_apply=%region_3.4 | all-reduce | flops 6144 | bytes 36864 | tf_op jit(solution)/shard_map/psum | solution.py:58
  137.3 0.1 subtract_multiply_fusion
  137.4 1.1 reshape.74
  138.5 1.6 fusion.28
  140.1 0.3 convolution_bitcast_fusion.1
  140.4 0.0 copy-done.1
  140.4 1.6 fusion
  142.1 0.2 copy.84
  142.3 1.7 gather_fusion.1
  143.9 1.3 fusion.26
  145.2 0.8 reshape.98
  146.0 6.6 %all-to-all-start.1 = ((bf16[128,2,128]{2,1,0:T(2,128)(2,1)}), bf16[128,2,128]{2,1,0:T(2,128)(2,1)S(1)}, u32[]{:S(2)}, u32[]{:S(2)}) async-start(bf16[128,2,128]{2,1,0:T(2,128)(2,1)} %reshape.98), calls=%async_computation.1 | async-start | bytes 131072 | tf_op jit(solution)/shard_map/all_to_all | solution.py:93
  152.6 0.1 dynamic-slice_convert_fusion
  152.7 0.6 pad_maximum_fusion
  153.3 10.0 %all-to-all-done.1 = bf16[128,2,128]{2,1,0:T(2,128)(2,1)S(1)} async-done(((bf16[128,2,128]{2,1,0:T(2,128)(2,1)}), bf16[128,2,128]{2,1,0:T(2,128)(2,1)S(1)}, u32[]{:S(2)}, u32[]{:S(2)}) %all-to-all-start.1) | async-done | bytes 65568 | tf_op jit(solution)/shard_map/all_to_all | solution.py:93
  163.3 0.2 reshape.99
  163.4 0.1 copy.85
  163.6 0.9 copy.86
  164.5 2.2 %copy.87 = f32[128,4,2,32]{3,1,0,2:T(4,128)} copy(f32[128,4,2,32]{3,2,0,1:T(2,128)} %bitcast.50) | data formatting | bytes 262144 | tf_op jit(solution)/shard_map/convert_element_type | solution.py:94
  166.7 1.2 copy.88
  167.9 0.7 divide_convert_fusion
  (8 shorter events, 0.1 us)
Async XLA Ops:
  0.6 77.8 %copy-start = (bf16[1024,1536]{1,0:T(8,128)(2,1)S(1)}, bf16[1024,1536]{1,0:T(8,128)(2,1)}, u32[]{:S(2)}) copy-start(bf16[1024,1536]{1,0:T(8,128)(2,1)} %param.15) | copy-start | bytes 9437188
  0.6 35.1 %copy-start.3 = (bf16[256,8]{0,1:T(8,128)(2,1)S(1)}, bf16[256,8]{0,1:T(8,128)(2,1)}, u32[]{:S(2)}) copy-start(bf16[256,8]{0,1:T(8,128)(2,1)} %param.16) | copy-start | bytes 12292
  0.7 35.2 %copy-start.4 = (bf16[256,8]{0,1:T(8,128)(2,1)S(1)}, bf16[256,8]{0,1:T(8,128)(2,1)}, u32[]{:S(2)}) copy-start(bf16[256,8]{0,1:T(8,128)(2,1)} %param.12) | copy-start | bytes 12292
  0.7 74.8 %copy-start.2 = (f32[2048]{0:T(1024)S(1)}, f32[2048]{0:T(1024)}, u32[]{:S(2)}) copy-start(f32[2048]{0:T(1024)} %param.13) | copy-start | bytes 24580
  3.5 28.4 %all-to-all-start = ((bf16[128,2,128]{2,1,0:T(2,128)(2,1)}), bf16[128,2,128]{2,1,0:T(2,128)(2,1)S(1)}, u32[]{:S(2)}, u32[]{:S(2)}) async-start(bf16[128,2,128]{2,1,0:T(2,128)(2,1)} %reshape.96), calls=%async_computation | async-start | bytes 131072 | tf_op jit(solution)/shard_map/all_to_all | solution.py:34
  78.9 61.5 %copy-start.1 = (f32[4,256,32]{1,2,0:T(8,128)S(1)}, f32[4,256,32]{1,2,0:T(8,128)}, u32[]{:S(2)}) copy-start(f32[4,256,32]{1,2,0:T(8,128)} %convolution_bitcast_fusion) | copy-start | bytes 393220
  146.0 17.3 %all-to-all-start.1 = ((bf16[128,2,128]{2,1,0:T(2,128)(2,1)}), bf16[128,2,128]{2,1,0:T(2,128)(2,1)S(1)}, u32[]{:S(2)}, u32[]{:S(2)}) async-start(bf16[128,2,128]{2,1,0:T(2,128)(2,1)} %reshape.98), calls=%async_computation.1 | async-start | bytes 131072 | tf_op jit(solution)/shard_map/all_to_all | solution.py:93
where the time goes:
time: 169 us
  blocking collectives  90.6 us (54%)
  starting transfers between devices  24.4 us (14%)
  waiting for transfers between devices  16 us (9%)
  local copies, waits for them, and re-layouts  15.2 us (9%)
  matrix products  13.2 us (8%)
  other arithmetic  8.46 us (5%)
    psum x1, blocking collectives, shards(): gram_block = lax.psum(gram_local, 'tensor')  36.7 us
    psum x1, blocking collectives, shards(): summed = lax.psum(partial_out, 'tensor')  32.2 us
    psum x1, blocking collectives, shards(): lax.psum(jnp.dot(d_up, up_weight.T, preferred_element_type=jnp.float32).a...  21.8 us
    all_to_all x1, starting transfers between devices, shards(): lax.all_to_all(pooled, 'dp', split_axis=0, concat_axis=1, tiled=True)  17.8 us
    all_to_all x1, waiting for transfers between devices, shards(): lax.all_to_all(d_slots, 'dp', split_axis=1, concat_axis=0, tiled=True)  9.97 us
    all_to_all x1, starting transfers between devices, shards(): lax.all_to_all(d_slots, 'dp', split_axis=1, concat_axis=0, tiled=True)  6.59 us
    all_to_all x1, waiting for transfers between devices, shards(): lax.all_to_all(pooled, 'dp', split_axis=0, concat_axis=1, tiled=True)  6.02 us
    convert_element_type x3, local copies, waits for them, and re-layouts, shards(): grad_sums = (d_pooled.astype(jnp.float32) / lengths).astype(jnp.bfloat16)  4.34 us
  transfers between devices with their start and end apart: 2, of which 2 were waited for; matrix products, arithmetic and copies ran while one was open for 3% of the time, Pallas kernels for 0%

commit v1 on v0

v1 whole, which is shorter than its diff:
```python
import jax
import jax.numpy as jnp
from jax import lax
from jax.experimental import pallas as pl
from jax.experimental.pallas import tpu as pltpu
from jax.sharding import PartitionSpec as P

F = 256
D = 192
K = 8
NF = 8
S = 4
DW = 32
TP = 6
DP = 128
H = 1024
FK = F * K
ROW = 2 * DW * S
bf16 = jnp.bfloat16
f32 = jnp.float32

VMEM = pl.BlockSpec(memory_space=pltpu.VMEM)


def iota(shape, dim):
    return lax.broadcasted_iota(jnp.int32, shape, dim)


def dot(a, b):
    return jnp.dot(a, b, preferred_element_type=f32)


def dot_nt(a, b):
    return lax.dot_general(a, b, (((1,), (1,)), ((), ())), preferred_element_type=f32)


def split(x):
    hi = x.astype(bf16)
    return hi, (x - hi.astype(f32)).astype(bf16)


def swap_pair(x):
    n = x.shape[1]
    first = (iota(x.shape, 1) // DW) % 2 == 0
    return jnp.where(first, pltpu.roll(x, n - DW, 1), pltpu.roll(x, DW, 1))


def pool_kernel(sums_ref, len_ref, out_ref, scr):
    parts = []
    for j in range(2):
        parts.append(sums_ref[j].astype(f32) / len_ref[j : j + 1, :].astype(f32))
    scr[...] = jnp.concatenate(parts, axis=0).T
    even = scr[pl.ds(0, 256, stride=2), :]
    odd = scr[pl.ds(1, 256, stride=2), :]
    out_ref[...] = jnp.concatenate([even, odd], axis=1).astype(bf16)


def prep_kernel(slot_ref, slot8_ref, fmlc_ref, cot_ref, cotl_ref, ow_ref, vt_ref, v_ref, r_ref, dh_ref, cotb_ref):
    row = iota((F, F), 0)
    place = 2 * (row % DP) + row // DP
    onehot = jnp.where(slot_ref[...] == place, 1.0, 0.0).astype(bf16)
    picked = dot(onehot, fmlc_ref[...])
    a, b = picked[:DP], picked[DP:]
    v_ref[...] = jnp.concatenate(
        [a[:, :K], b[:, :K], a[:, :K], b[:, :K], a[:, K:], b[:, K:]], axis=1
    ).astype(bf16)
    vt_ref[...] = jnp.concatenate([a.T, b.T], axis=0).astype(bf16)
    row8 = iota((F, FK), 0)
    place8 = 2 * (row8 % DP) + row8 // DP
    r_ref[...] = jnp.where(slot8_ref[...] == place8, 1.0, 0.0).astype(bf16)
    dh_ref[...] = dot_nt(cot_ref[...], ow_ref[...])
    c = cotl_ref[...]
    first = (iota(c.shape, 1) // DW) % 2 == 0
    zero = jnp.zeros_like(c)
    cotb_ref[...] = jnp.concatenate([jnp.where(first, c, zero), jnp.where(first, zero, c)], axis=0).astype(bf16)


def own_mask():
    shape = (2 * S * K, ROW)
    r, c = iota(shape, 0), iota(shape, 1)
    return ((r // K) % S == c // (2 * DW)) & (r // (S * K) == (c // DW) % 2)


def gram_kernel(x_ref, vt_ref, g_ref, x_out, cb_ref, lin_ref, scr):
    scr[...] = x_ref[...].astype(f32)
    x = jnp.concatenate(
        [scr[pl.ds(0, DP, stride=2), :], scr[pl.ds(1, DP, stride=2), :]], axis=1
    ).astype(bf16)
    x_out[...] = x
    y = dot(vt_ref[...], x)
    first = (iota((16, ROW), 1) // DW) % 2 == 0
    y = jnp.where(first, y[:16], y[16:])
    y = y + swap_pair(y)
    for s in range(S):
        lin_ref[s] = y[K:, s * 2 * DW : s * 2 * DW + DW].astype(bf16)
    tiled = jnp.concatenate([y[:K]] * (2 * S), axis=0)
    hi, lo = split(jnp.where(own_mask(), tiled, 0.0))
    cb = jnp.concatenate([hi, lo], axis=0)
    cb_ref[...] = cb
    g = dot_nt(cb, x)
    g = (g[:64] + g[64:]).astype(bf16)
    for t in range(TP):
        g_ref[t] = g


def mlp_kernel(g_ref, r_ref, gain_ref, up_ref, ow_ref, dh_ref, c_ref, wh_ref, sc_ref):
    g = g_ref[0].astype(f32)
    for t in range(1, TP):
        g = g + g_ref[t].astype(f32)
    hi, lo = split(jnp.concatenate([g[:32], g[32:]], axis=1))
    m = dot(jnp.concatenate([hi, lo], axis=0), r_ref[...])
    m = m[:32] + m[32:]
    same = iota(m.shape, 0) % K == iota(m.shape, 1) % K
    flat = jnp.sum(jnp.where(same, m, 0.0).reshape(S, K, FK), axis=1)
    centered = flat - jnp.mean(flat, axis=1, keepdims=True)
    scale = lax.rsqrt(jnp.mean(centered * centered, axis=1, keepdims=True) + 1e-05)
    whitened = centered * scale
    wh_ref[...] = whitened
    sc_ref[...] = jnp.broadcast_to(scale, sc_ref.shape)
    normed = (whitened * gain_ref[...]).astype(bf16)
    up = dot(normed, up_ref[...])
    sig = jax.nn.sigmoid(up)
    hidden = (up * sig).astype(bf16)
    d_up = (dh_ref[...] * (sig + up * sig * (1.0 - sig))).astype(bf16)
    fm = dot(hidden, ow_ref[...])
    d_norm = dot_nt(d_up, up_ref[...]).astype(bf16)
    for t in range(TP):
        c_ref[t, :, :FK] = d_norm
        c_ref[t, :, FK:] = jnp.concatenate(
            [fm[:, n * D + t * DW : n * D + (t + 1) * DW] for n in range(NF)], axis=1
        ).astype(bf16)


def grad_kernel(c_ref, r_ref, gain_ref, wh_ref, sc_ref, x_ref, cb_ref, v_ref, cotb_ref, z_ref, fm_ref, scr):
    c = c_ref[0].astype(f32)
    for t in range(1, TP):
        c = c + c_ref[t].astype(f32)
    fm_ref[...] = c[:, FK:]
    wh = wh_ref[...]
    gb = c[:, :FK] * gain_ref[...]
    flat = sc_ref[:, :1] * (
        gb
        - jnp.mean(gb, axis=1, keepdims=True)
        - wh * jnp.mean(gb * wh, axis=1, keepdims=True)
    )
    spread = jnp.broadcast_to(flat[:, None, :], (S, K, FK)).reshape(S * K, FK)
    same = iota(spread.shape, 0) % K == iota(spread.shape, 1) % K
    hi, lo = split(jnp.where(same, spread, 0.0))
    dg = dot_nt(jnp.concatenate([hi, lo], axis=0), r_ref[...])
    dg = dg[:32] + dg[32:]
    dg = jnp.concatenate([dg[:, :DP], dg[:, DP:]], axis=0)
    hi, lo = split(dg)
    x = x_ref[...]
    dc = dot(jnp.concatenate([hi, lo], axis=0), x)
    dc = jnp.where(own_mask(), dc[:64] + dc[64:], 0.0)
    dc = jnp.sum(dc.reshape(2 * S, K, ROW), axis=0)
    dc = dc + swap_pair(dc)
    first = (iota(dc.shape, 1) // DW) % 2 == 0
    zero = jnp.zeros_like(dc)
    dhi, dlo = split(jnp.concatenate([jnp.where(first, dc, zero), jnp.where(first, zero, dc)], axis=0))
    thi, tlo = split(dg.T)
    left = jnp.concatenate([thi, thi, tlo, v_ref[...]], axis=1)
    cb = cb_ref[...]
    right = jnp.concatenate([cb, cb[:64], dhi, dlo, cotb_ref[...]], axis=0)
    z = dot(left, right)
    scr[pl.ds(0, DP, stride=2), :] = z[:, :128]
    scr[pl.ds(1, DP, stride=2), :] = z[:, 128:]
    z_ref[...] = scr[...].astype(bf16)


def unpool_kernel(z_ref, len_ref, out_ref, scr):
    z = z_ref[...].astype(f32)
    scr[pl.ds(0, 256, stride=2), :] = z[:, :64]
    scr[pl.ds(1, 256, stride=2), :] = z[:, 64:]
    zt = scr[...].T
    for j in range(2):
        out_ref[j] = (zt[j * DW : (j + 1) * DW] / len_ref[j : j + 1, :].astype(f32)).astype(bf16)


def call(kernel, outs, args, scratch=(), name=None, cost=None):
    many = len(outs) > 1
    shapes = [jax.ShapeDtypeStruct(s, d) for s, d in outs]
    return pl.pallas_call(
        kernel,
        out_shape=shapes if many else shapes[0],
        in_specs=[VMEM] * len(args),
        out_specs=[VMEM] * len(outs) if many else VMEM,
        scratch_shapes=list(scratch),
        compiler_params=pltpu.CompilerParams(vmem_limit_bytes=8 * 2**20),
        name=name,
        cost_estimate=cost,
    )(*args)


def exchange(x, axis):
    return lax.all_to_all(x, axis, split_axis=0, concat_axis=0, tiled=True)


def shards(
    table_sums,
    bag_lengths,
    feature_slot,
    fm_project,
    ln_gain,
    up_weight,
    out_weight,
    lc_weight,
    cotangent,
):
    sums_t = jnp.transpose(table_sums, (1, 2, 0))
    len_t = jnp.transpose(bag_lengths, (1, 0))
    pooled = call(
        pool_kernel, [((256, 128), bf16)], (sums_t, len_t), [pltpu.VMEM((512, 64), f32)], "pool"
    )
    arrived = exchange(pooled.reshape(DP, 2, 128), "dp").reshape(256, 128)

    slot = feature_slot.reshape(1, F)
    slot8 = jnp.repeat(feature_slot, K).reshape(1, FK)
    fmlc = jnp.concatenate([fm_project, lc_weight], axis=1)
    gain = ln_gain.reshape(1, FK)
    cot_fm = cotangent[:, :NF].reshape(S, NF * D)
    offset = lax.axis_index("tensor") * DW
    cot_l = lax.dynamic_slice_in_dim(cotangent[:, NF:], offset, DW, 2).astype(f32)
    cot_l = jnp.transpose(cot_l, (1, 0, 2))[:, :, None, :]
    cot_l = jnp.broadcast_to(cot_l, (K, S, 2, DW)).reshape(K, ROW)
    vt, v, r, dh, cotb = call(
        prep_kernel,
        [((32, DP), bf16), ((DP, 48), bf16), ((F, FK), bf16), ((S, H), f32), ((16, ROW), bf16)],
        (slot, slot8, fmlc, cot_fm, cot_l, out_weight),
        name="prep",
    )
    g6, x, cb, lin = call(
        gram_kernel,
        [((TP, 64, DP), bf16), ((DP, ROW), bf16), ((128, ROW), bf16), ((S, K, DW), bf16)],
        (arrived, vt),
        [pltpu.VMEM((256, 128), f32)],
        "gram",
    )
    g6 = exchange(g6, "tensor")
    c6, wh, sc = call(
        mlp_kernel,
        [((TP, S, FK + NF * DW), bf16), ((S, FK), f32), ((S, 128), f32)],
        (g6, r, gain, up_weight, out_weight, dh),
        name="mlp",
    )
    c6 = exchange(c6, "tensor")
    z, fm = call(
        grad_kernel,
        [((256, 128), bf16), ((S, NF * DW), f32)],
        (c6, r, gain, wh, sc, x, cb, v, cotb),
        [pltpu.VMEM((256, 128), f32)],
        "grad",
    )
    back = exchange(z.reshape(DP, 2, 128), "dp").reshape(256, 128)
    grad_t = call(
        unpool_kernel, [((2, DW, 512), bf16)], (back, len_t), [pltpu.VMEM((512, 64), f32)], "unpool"
    )
    layer_out = jnp.concatenate([fm.reshape(S, NF, DW).astype(bf16), lin], axis=1)
    return (layer_out, jnp.transpose(grad_t, (2, 0, 1)))


def solution(mesh):
    return jax.shard_map(
        shards,
        mesh=mesh,
        in_specs=(
            P(None, "dp", "tensor"),
            P(None, "dp"),
            P(),
            P(),
            P(),
            P(None, "tensor"),
            P("tensor", None),
            P(),
            P("dp", None, None),
        ),
        out_specs=(P("dp", None, "tensor"), P(None, "dp", "tensor")),
        check_vma=False,
    )
```

time: 169 us -> 97.2 us (0.58)
  blocking collectives: 90.6 us -> 36 us
  matrix products: 13.2 us -> 0 us
  Pallas kernels: 0 us -> 7.31 us
  other arithmetic: 8.46 us -> 1.41 us
  local copies, waits for them, and re-layouts: 15.2 us -> 10.6 us
  starting transfers between devices: 24.4 us -> 27.4 us
  waiting for transfers between devices: 16 us -> 13.2 us
    psum x3 -> x0, blocking collectives: 90.6 us -> none  [the longest x1 36.7 us: shards(): gram_block = lax.psum(gram_local, 'tensor')]
    all_to_all x0 -> x2, blocking collectives: none -> 36 us  [exchange(): return lax.all_to_all(x, axis, split_axis=0, concat_axis=0, tiled=True)]
    dot_general x10 -> x0, matrix products: 13.2 us -> none  [the longest x1 4.22 us: shards(): jnp.dot(d_up, up_weight.T, preferred_element_type=jnp.float32)]
    pallas_call x0 -> x6, Pallas kernels: none -> 7.31 us  [call(): pl.pallas_call(kernel, out_shape=shapes if many else shapes[0], in_specs=...]
    unnamed x14 -> x22, local copies, waits for them, and re-layouts: 1.94 us -> 8.53 us
    convert_element_type x4 -> x1, local copies, waits for them, and re-layouts: 4.5 us -> 0.08 us  [shards(): fm.reshape(S, NF, DW).astype(bf16)]
    gather x2 -> x0, local copies, waits for them, and re-layouts: 3.31 us -> none  [the longest x1 1.66 us: shards(): d_slots = jnp.take(embedding_gradient, inverse, axis=1).astype(jnp.bfloat16)]
    all_to_all x2, starting transfers between devices: 24.4 us -> 27.4 us  [exchange(): return lax.all_to_all(x, axis, split_axis=0, concat_axis=0, tiled=True)]
  transfers between devices with their start and end apart: 2 -> 2, of which waited for: 2 -> 2; matrix products, arithmetic and copies ran while one was open for 3% -> 4% of each run, Pallas kernels for 0% -> 1%
where the time goes in v1:
time: 97.2 us; the launch traced here: 96.6 us
  blocking collectives  36 us (37%)
  starting transfers between devices  27.4 us (28%)
  waiting for transfers between devices  13.2 us (14%)
  local copies, waits for them, and re-layouts  10.6 us (11%)
  Pallas kernels  7.31 us (8%)
  other arithmetic  1.41 us (1%)
    all_to_all x2, blocking collectives, exchange(): return lax.all_to_all(x, axis, split_axis=0, concat_axis=0, tiled=True)  36 us
    all_to_all x2, starting transfers between devices, exchange(): return lax.all_to_all(x, axis, split_axis=0, concat_axis=0, tiled=True)  27.4 us
    all_to_all x2, waiting for transfers between devices, exchange(): return lax.all_to_all(x, axis, split_axis=0, concat_axis=0, tiled=True)  13.2 us
    unnamed x22, local copies, waits for them, and re-layouts  8.53 us
    pallas_call x6, Pallas kernels, call(): pl.pallas_call(kernel, out_shape=shapes if many else shapes[0], in_specs=...  7.31 us
  transfers between devices with their start and end apart: 2, of which 2 were waited for; matrix products, arithmetic and copies ran while one was open for 4% of the time, Pallas kernels for 1%

profile of v1, /device:TPU:1, one launch (start us, length us, event | category | flops | bytes accessed | tf_op | source)
XLA Modules:
  0.0 96.6 jit_solution(7696887183648860023)
XLA Ops:
  0.6 0.0 copy-start.6
  0.6 0.8 copy-done.6
  1.5 0.0 copy-start.8
  1.5 0.7 copy-done.8
  2.2 0.0 copy-start.7
  2.2 0.9 pool.1
  3.0 17.8 %all-to-all-start = ((bf16[128,2,128]{2,1,0:T(2,128)(2,1)}), bf16[128,2,128]{2,1,0:T(2,128)(2,1)S(1)}, u32[]{:S(2)}, u32[]{:S(2)}) async-start(bf16[128,2,128]{2,1,0:T(2,128)(2,1)} %bitcast.2), calls=%async_computation | async-start | bytes 131072 | tf_op jit(solution)/shard_map/all_to_all | solution.py:196
  20.8 0.7 fusion
  21.6 0.1 convert_bitcast_fusion
  21.7 0.1 reshape.34.cot_ref
  21.8 0.1 reshape.35.cotl_ref
  21.9 0.7 pad_maximum_fusion.1
  22.6 0.1 copy.18.fmlc_ref
  22.7 0.8 broadcast_in_dim.4
  23.5 0.1 reshape_reshape.3.slot8_ref
  23.6 0.0 copy-start
  23.6 1.9 %copy-done = bf16[1024,1536]{1,0:T(8,128)(2,1)S(1)} copy-done((bf16[1024,1536]{1,0:T(8,128)(2,1)S(1)}, bf16[1024,1536]{1,0:T(8,128)(2,1)}, u32[]{:S(2)}) %copy-start) | copy-done | bytes 3145752
  25.5 0.0 copy-start.10
  25.5 0.7 copy-done.10
  26.2 0.0 copy-start.1
  26.2 1.1 %prep.1 = (bf16[32,128]{1,0:T(8,128)(2,1)S(1)}, bf16[128,48]{1,0:T(8,128)(2,1)S(1)}, bf16[256,2048]{1,0:T(8,128)(2,1)S(1)}, f32[4,1024]{1,0:T(4,128)S(1)}, bf16[16,256]{1,0:T(8,128)(2,1)S(1)}) custom-call(s32[1,256]{1,0:T(1,128)S(1)} %bitcast.18, s32[1,2048]{1,0:T(1,128)S(1)} %reshape_reshape.3.slot8_ref, bf16[256,16]{1,0:T(8,128)(2,1)S(1)} %copy.18.fmlc_ref, ...), custom_call_target="tpu_custom_call" | custom-call | tf_op jit(solution)/shard_map/prep/pallas_call | solution.py:183
  27.2 0.0 copy-start.3
  27.2 1.0 %copy-done.3 = bf16[256,2048]{1,0:T(8,128)(2,1)} copy-done((bf16[256,2048]{1,0:T(8,128)(2,1)}, bf16[256,2048]{1,0:T(8,128)(2,1)S(1)}, u32[]{:S(2)}) %copy-start.3) | copy-done | bytes 1048600
  28.2 3.2 %all-to-all-done = bf16[128,2,128]{2,1,0:T(2,128)(2,1)S(1)} async-done(((bf16[128,2,128]{2,1,0:T(2,128)(2,1)}), bf16[128,2,128]{2,1,0:T(2,128)(2,1)S(1)}, u32[]{:S(2)}, u32[]{:S(2)}) %all-to-all-start) | async-done | bytes 65568 | tf_op jit(solution)/shard_map/all_to_all | solution.py:196
  31.5 0.4 gram.1
  31.9 22.4 %all_to_all.20.g_ref = bf16[6,64,128]{2,1,0:T(8,128)(2,1)S(1)} all-to-all(bf16[6,64,128]{2,1,0:T(8,128)(2,1)S(1)} %get-tuple-element.17), channel_id=1, replica_groups=mesh['dp'=128,'tensor'=6] {'tensor'}, dimensions={0} | all-to-all | bytes 196608 | tf_op jit(solution)/shard_map/all_to_all | solution.py:196
  54.2 0.0 copy-done.7
  54.2 0.0 copy-done.1
  54.2 0.0 copy-start.2
  54.2 2.2 %copy-done.2 = bf16[2048,1024]{1,0:T(8,128)(2,1)S(1)} copy-done((bf16[2048,1024]{1,0:T(8,128)(2,1)S(1)}, bf16[2048,1024]{1,0:T(8,128)(2,1)}, u32[]{:S(2)}) %copy-start.2) | copy-done | bytes 4194328
  56.4 0.0 copy-start.4
  56.4 1.2 %copy-done.4 = bf16[256,2048]{1,0:T(8,128)(2,1)S(1)} copy-done((bf16[256,2048]{1,0:T(8,128)(2,1)S(1)}, bf16[256,2048]{1,0:T(8,128)(2,1)}, u32[]{:S(2)}) %copy-start.4) | copy-done | bytes 1048600
  57.7 0.0 copy-start.5
  57.7 0.0 copy-start.9
  57.7 2.6 %mlp.1 = (bf16[6,4,2304]{2,1,0:T(4,128)(2,1)S(1)}, f32[4,2048]{1,0:T(4,128)S(1)}, f32[4,128]{1,0:T(4,128)S(1)}) custom-call(bf16[6,64,128]{2,1,0:T(8,128)(2,1)S(1)} %all_to_all.20.g_ref, bf16[256,2048]{1,0:T(8,128)(2,1)S(1)} %copy-done.4, f32[1,2048]{1,0:T(1,128)S(1)} %bitcast.14, bf16[2048,1024]{1,0:T(8,128)(2,1)S(1)} %copy-done.2, ...), custom_call_target="tpu_custom_call" | custom-call | tf_op jit(solution)/shard_map/mlp/pallas_call | solution.py:183
  60.3 13.6 %all_to_all.21.c_ref = bf16[6,4,2304]{2,1,0:T(4,128)(2,1)S(1)} all-to-all(bf16[6,4,2304]{2,1,0:T(4,128)(2,1)S(1)} %get-tuple-element.20), channel_id=1, replica_groups=mesh['dp'=128,'tensor'=6] {'tensor'}, dimensions={0} | all-to-all | bytes 221184 | tf_op jit(solution)/shard_map/all_to_all | solution.py:196
  73.9 0.0 copy-done.5
  73.9 1.6 %grad.1 = (bf16[256,128]{1,0:T(8,128)(2,1)}, f32[4,256]{1,0:T(4,128)S(1)}) custom-call(bf16[6,4,2304]{2,1,0:T(4,128)(2,1)S(1)} %all_to_all.21.c_ref, bf16[256,2048]{1,0:T(8,128)(2,1)S(1)} %copy-done.5, f32[1,2048]{1,0:T(1,128)S(1)} %bitcast.15, f32[4,2048]{1,0:T(4,128)S(1)} %get-tuple-element.21.wh_ref, f32[4,128]{1,0:T(4,128)S(1)} %get-tuple-element.22.sc_ref, ...), custom_call_target="tpu_custom_call" | custom-call | tf_op jit(solution)/shard_map/grad/pallas_call | solution.py:183
  75.5 9.6 %all-to-all-start.3 = ((bf16[128,2,128]{2,1,0:T(2,128)(2,1)}), bf16[128,2,128]{2,1,0:T(2,128)(2,1)S(1)}, u32[]{:S(2)}, u32[]{:S(2)}) async-start(bf16[128,2,128]{2,1,0:T(2,128)(2,1)} %bitcast.7), calls=%async_computation.3 | async-start | bytes 131072 | tf_op jit(solution)/shard_map/all_to_all | solution.py:196
  85.1 0.1 convert_element_type.8
  85.2 0.6 pad_maximum_fusion
  85.8 10.0 %all-to-all-done.3 = bf16[128,2,128]{2,1,0:T(2,128)(2,1)S(1)} async-done(((bf16[128,2,128]{2,1,0:T(2,128)(2,1)}), bf16[128,2,128]{2,1,0:T(2,128)(2,1)S(1)}, u32[]{:S(2)}, u32[]{:S(2)}) %all-to-all-start.3) | async-done | bytes 65568 | tf_op jit(solution)/shard_map/all_to_all | solution.py:196
  95.8 0.0 copy-done.9
  95.8 0.8 unpool.1
  (3 shorter events, 0.0 us)
Async XLA Ops:
  0.6 0.8 copy-start.6
  1.5 0.7 copy-start.8
  2.2 52.1 %copy-start.7 = (f32[2048]{0:T(1024)S(1)}, f32[2048]{0:T(1024)}, u32[]{:S(2)}) copy-start(f32[2048]{0:T(1024)} %param.13) | copy-start | bytes 24580
  3.0 28.4 %all-to-all-start = ((bf16[128,2,128]{2,1,0:T(2,128)(2,1)}), bf16[128,2,128]{2,1,0:T(2,128)(2,1)S(1)}, u32[]{:S(2)}, u32[]{:S(2)}) async-start(bf16[128,2,128]{2,1,0:T(2,128)(2,1)} %bitcast.2), calls=%async_computation | async-start | bytes 131072 | tf_op jit(solution)/shard_map/all_to_all | solution.py:196
  23.6 1.9 %copy-start = (bf16[1024,1536]{1,0:T(8,128)(2,1)S(1)}, bf16[1024,1536]{1,0:T(8,128)(2,1)}, u32[]{:S(2)}) copy-start(bf16[1024,1536]{1,0:T(8,128)(2,1)} %ow_ref.3) | copy-start | bytes 9437188
  25.5 0.7 copy-start.10
  26.2 28.1 %copy-start.1 = (bf16[1024,1536]{1,0:T(8,128)(2,1)S(1)}, bf16[1024,1536]{1,0:T(8,128)(2,1)}, u32[]{:S(2)}) copy-start(bf16[1024,1536]{1,0:T(8,128)(2,1)} %ow_ref.3) | copy-start | bytes 9437188
  27.2 1.0 %copy-start.3 = (bf16[256,2048]{1,0:T(8,128)(2,1)}, bf16[256,2048]{1,0:T(8,128)(2,1)S(1)}, u32[]{:S(2)}) copy-start(bf16[256,2048]{1,0:T(8,128)(2,1)S(1)} %get-tuple-element.18.r_ref) | copy-start | bytes 3145732
  54.2 2.2 %copy-start.2 = (bf16[2048,1024]{1,0:T(8,128)(2,1)S(1)}, bf16[2048,1024]{1,0:T(8,128)(2,1)}, u32[]{:S(2)}) copy-start(bf16[2048,1024]{1,0:T(8,128)(2,1)} %up_ref.1) | copy-start | bytes 12582916
  56.4 1.2 %copy-start.4 = (bf16[256,2048]{1,0:T(8,128)(2,1)S(1)}, bf16[256,2048]{1,0:T(8,128)(2,1)}, u32[]{:S(2)}) copy-start(bf16[256,2048]{1,0:T(8,128)(2,1)} %copy-done.3) | copy-start | bytes 3145732
  57.7 16.2 %copy-start.5 = (bf16[256,2048]{1,0:T(8,128)(2,1)S(1)}, bf16[256,2048]{1,0:T(8,128)(2,1)}, u32[]{:S(2)}) copy-start(bf16[256,2048]{1,0:T(8,128)(2,1)} %copy-done.3) | copy-start | bytes 3145732
  57.7 38.1 %copy-start.9 = (s32[512,2]{0,1:T(2,128)S(1)}, s32[512,2]{0,1:T(2,128)}, u32[]{:S(2)}) copy-start(s32[512,2]{0,1:T(2,128)} %param.10) | copy-start | bytes 12292
  75.5 20.3 %all-to-all-start.3 = ((bf16[128,2,128]{2,1,0:T(2,128)(2,1)}), bf16[128,2,128]{2,1,0:T(2,128)(2,1)S(1)}, u32[]{:S(2)}, u32[]{:S(2)}) async-start(bf16[128,2,128]{2,1,0:T(2,128)(2,1)} %bitcast.7), calls=%async_computation.3 | async-start | bytes 131072 | tf_op jit(solution)/shard_map/all_to_all | solution.py:196

commit v2 on v1

v2 whole, which is shorter than its diff:
```python
import jax
import jax.numpy as jnp
from jax import lax
from jax.experimental import pallas as pl
from jax.experimental.pallas import tpu as pltpu
from jax.sharding import PartitionSpec as P

F = 256
D = 192
K = 8
NF = 8
S = 4
DW = 32
TP = 6
DP = 128
H = 1024
FK = F * K
ROW = DW * S
LARGE = 53_000_000
WHOLE = 66_600_000
CUT = 1024
bf16 = jnp.bfloat16
f32 = jnp.float32

VMEM = pl.BlockSpec(memory_space=pltpu.VMEM)
SMEM = pl.BlockSpec(memory_space=pltpu.SMEM)
HBM = pl.BlockSpec(memory_space=pltpu.HBM)


def iota(shape, dim):
    return lax.broadcasted_iota(jnp.int32, shape, dim)


def dot(a, b):
    return jnp.dot(a, b, preferred_element_type=f32)


def dot_nt(a, b):
    return lax.dot_general(a, b, (((1,), (1,)), ((), ())), preferred_element_type=f32)


def split(x):
    hi = x.astype(bf16)
    return hi, (x - hi.astype(f32)).astype(bf16)


def rows(parts):
    return jnp.concatenate(parts, axis=0)


def lanes(parts):
    return jnp.concatenate(parts, axis=1)


def own_sample():
    shape = (S * K, ROW)
    return iota(shape, 0) // K == iota(shape, 1) // DW


def expander():
    shape = (32, 256)
    return jnp.where(iota(shape, 0) == iota(shape, 1) // K, 1.0, 0.0).astype(bf16)


def own_rank():
    shape = (256, 256)
    return iota(shape, 0) % K == iota(shape, 1) % K


def pool_kernel(sums_hbm, len_hbm, out_ref, sums_ref, len_ref, scr, pairs, sem):
    sums_copy = pltpu.make_async_copy(sums_hbm, sums_ref, sem.at[0])
    len_copy = pltpu.make_async_copy(len_hbm, len_ref, sem.at[1])
    sums_copy.start()
    len_copy.start()
    len_copy.wait()
    length = len_ref[...].astype(f32)
    sums_copy.wait()
    for j in range(2):
        scr[j] = (sums_ref[j].astype(f32) / length[j : j + 1]).T
        pairs[pl.ds(j, DP, stride=2), :] = lanes(
            [scr[j, pl.ds(s, DP, stride=S), :] for s in range(S)]
        )
    out_ref[...] = pairs[...].astype(bf16)


def slot_kernel(slot_ref, fm_ref, lc_ref, hot_ref, vt_ref):
    onehot = jnp.where(slot_ref[...] == iota((F, F), 0), 1.0, 0.0).astype(bf16)
    hot_ref[...] = onehot
    both = rows([fm_ref[...].astype(f32), lc_ref[...].astype(f32)]).astype(bf16)
    vt_ref[...] = dot_nt(both, onehot).astype(bf16)


def gram_kernel(x_ref, vt_ref, hot_ref, g_ref, x_out, cb_ref, lin_ref):
    x = x_ref[...]
    x_out[...] = x
    y = dot(vt_ref[...], x)
    for s in range(S):
        lin_ref[s] = y[K:, s * DW : (s + 1) * DW].astype(bf16)
    hi, lo = split(jnp.where(own_sample(), rows([y[:K]] * S), 0.0))
    cb = rows([hi, lo])
    cb_ref[...] = cb
    g = dot_nt(cb, x)
    g = (g[:32] + g[32:]).astype(bf16)
    g = dot(g, hot_ref[...]).astype(bf16)
    for t in range(TP):
        g_ref[t] = g


def prep_kernel(
    rank_ref, cot_ref, vt_ref, after_ref, up_hbm, ow_hbm, dh_ref, cotl_ref, v_ref, up_out, ow_ref, cot_scr, sem
):
    ow_copy = pltpu.make_async_copy(ow_hbm, ow_ref, sem.at[0])
    up_copy = pltpu.make_async_copy(up_hbm.at[pl.ds(0, CUT)], up_out, sem.at[1])
    ow_copy.start()
    up_copy.start()
    cot_scr[...] = cot_ref[...].astype(f32)
    vt = vt_ref[...].astype(f32)
    v = vt.T
    v_ref[...] = lanes([v[:, :K], v]).astype(bf16)
    rank = rank_ref[0]
    parts = []
    for s in range(S):
        block = cot_scr[s, NF:, :]
        own = jnp.zeros((K, DW), f32)
        for t in range(TP):
            own = jnp.where(rank == t, block[:, t * DW : (t + 1) * DW], own)
        parts.append(own)
    cotl_ref[...] = lanes(parts)
    cot_fm = lanes([cot_scr[:, n, :] for n in range(NF)]).astype(bf16)
    ow_copy.wait()
    dh_ref[...] = dot_nt(cot_fm, ow_ref[...])
    up_copy.wait()


def mlp_kernel(g_ref, gain_ref, dh_ref, lo_ref, up_hbm, ow_hbm, c_ref, wh_ref, sc_ref, hi_ref, ow_ref, sem):
    up_copy = pltpu.make_async_copy(up_hbm.at[pl.ds(CUT, FK - CUT)], hi_ref, sem.at[0])
    ow_copy = pltpu.make_async_copy(ow_hbm, ow_ref, sem.at[1])
    up_copy.start()
    ow_copy.start()
    g = g_ref[0].astype(f32)
    for t in range(1, TP):
        g = g + g_ref[t].astype(f32)
    g = rows([g[:, c * 32 : (c + 1) * 32] for c in range(8)])
    hi, lo = split(g)
    m = dot(rows([hi, lo]), expander())
    m = jnp.where(own_rank(), m[:256] + m[256:], 0.0)
    m = jnp.sum(m.reshape(8 * S, K, 256), axis=1)
    flat = lanes([m[c * S : (c + 1) * S] for c in range(8)])
    centered = flat - jnp.mean(flat, axis=1, keepdims=True)
    scale = lax.rsqrt(jnp.mean(centered * centered, axis=1, keepdims=True) + 1e-05)
    whitened = centered * scale
    wh_ref[...] = whitened
    sc_ref[...] = jnp.broadcast_to(scale, sc_ref.shape)
    normed = (whitened * gain_ref[...]).astype(bf16)
    up = dot(normed[:, :CUT], lo_ref[...])
    up_copy.wait()
    up = up + dot(normed[:, CUT:], hi_ref[...])
    sig = jax.nn.sigmoid(up)
    hidden = (up * sig).astype(bf16)
    d_up = (dh_ref[...] * (sig + up * sig * (1.0 - sig))).astype(bf16)
    d_lo = dot_nt(d_up, lo_ref[...]).astype(bf16)
    d_hi = dot_nt(d_up, hi_ref[...]).astype(bf16)
    ow_copy.wait()
    fm = dot(hidden, ow_ref[...])
    for t in range(TP):
        c_ref[t, :, :CUT] = d_lo
        c_ref[t, :, CUT:FK] = d_hi
        c_ref[t, :, FK:] = lanes(
            [fm[:, n * D + t * DW : n * D + (t + 1) * DW] for n in range(NF)]
        ).astype(bf16)


def grad_kernel(c_ref, gain_ref, wh_ref, sc_ref, x_ref, cb_ref, v_ref, cotl_ref, hot_ref, z_ref, fm_ref):
    c = c_ref[0].astype(f32)
    for t in range(1, TP):
        c = c + c_ref[t].astype(f32)
    fm_ref[...] = c[:, FK:]
    wh = wh_ref[...]
    gb = c[:, :FK] * gain_ref[...]
    flat = sc_ref[:, :1] * (
        gb
        - jnp.mean(gb, axis=1, keepdims=True)
        - wh * jnp.mean(gb * wh, axis=1, keepdims=True)
    )
    spread = rows(
        [
            jnp.broadcast_to(flat[:, None, c * 256 : (c + 1) * 256], (S, K, 256)).reshape(S * K, 256)
            for c in range(8)
        ]
    )
    hi, lo = split(jnp.where(own_rank(), spread, 0.0))
    dg = dot_nt(rows([hi, lo]), expander())
    dg = dg[:256] + dg[256:]
    dg = lanes([dg[c * 32 : (c + 1) * 32] for c in range(8)])
    hi, lo = split(dg)
    dg = dot_nt(rows([hi, lo]), hot_ref[...])
    dc = dot(dg.astype(bf16), x_ref[...])
    dc = jnp.where(own_sample(), dc[:32] + dc[32:], 0.0)
    dc = jnp.sum(dc.reshape(S, K, ROW), axis=0)
    dc_hi = dc.astype(bf16).astype(f32)
    cb = cb_ref[...].astype(f32)
    right = rows([cb[:32], cb[:32], cb[32:], dc_hi, dc - dc_hi, cotl_ref[...]]).astype(bf16)
    dgt = dg.T.astype(bf16)
    left = lanes([dgt, dgt[:, :32], v_ref[...]])
    z_ref[...] = dot(left, right).astype(bf16)


def unpool_kernel(z_ref, len_ref, out_ref, pairs, scr):
    pairs[...] = z_ref[...].astype(f32)
    for j in range(2):
        z = pairs[pl.ds(j, DP, stride=2), :]
        for s in range(S):
            scr[j, pl.ds(s, DP, stride=S), :] = z[:, s * DW : (s + 1) * DW]
        out_ref[j] = (scr[j].T / len_ref[j : j + 1, :].astype(f32)).astype(bf16)


def call(name, kernel, outs, args, specs=None, scratch=(), flops=0, nbytes=0, limit=16 * 2**20):
    many = len(outs) > 1
    shapes = [jax.ShapeDtypeStruct(s, d) for s, d in outs]
    return pl.pallas_call(
        kernel,
        out_shape=shapes if many else shapes[0],
        in_specs=specs or [VMEM] * len(args),
        out_specs=[VMEM] * len(outs) if many else VMEM,
        scratch_shapes=list(scratch),
        compiler_params=pltpu.CompilerParams(vmem_limit_bytes=limit),
        name=name,
        cost_estimate=pl.CostEstimate(flops=flops, bytes_accessed=nbytes, transcendentals=0)
        if flops
        else None,
    )(*args)


def exchange(x, axis):
    return lax.all_to_all(x, axis, split_axis=0, concat_axis=0, tiled=True)


def shards(
    table_sums,
    bag_lengths,
    feature_slot,
    fm_project,
    ln_gain,
    up_weight,
    out_weight,
    lc_weight,
    cotangent,
):
    samples = table_sums.shape[0]
    sums_t = jnp.transpose(table_sums, (1, 2, 0))
    len_t = jnp.transpose(bag_lengths, (1, 0))
    dma = pltpu.SemaphoreType.DMA
    pooled = call(
        "pool",
        pool_kernel,
        [((F, ROW), bf16)],
        (sums_t, len_t),
        [HBM, HBM],
        [
            pltpu.VMEM((2, DW, samples), bf16),
            pltpu.VMEM((2, samples), jnp.int32),
            pltpu.VMEM((2, samples, DW), f32),
            pltpu.VMEM((F, ROW), f32),
            dma((2,)),
        ],
        limit=WHOLE,
    )
    arrived = exchange(pooled.reshape(DP, 2, ROW), "dp").reshape(F, ROW)
    hot, vt = call(
        "slots",
        slot_kernel,
        [((F, F), bf16), ((2 * K, F), bf16)],
        (feature_slot.reshape(1, F), fm_project.T, lc_weight.T),
    )
    g6, x, cb, lin = call(
        "gram",
        gram_kernel,
        [((TP, S * K, F), bf16), ((F, ROW), bf16), ((2 * S * K, ROW), bf16), ((S, K, DW), bf16)],
        (arrived, vt, hot),
    )
    g6 = exchange(g6, "tensor")
    rank = lax.axis_index("tensor").astype(jnp.int32).reshape(1)
    dh, cotl, v, up_lo = call(
        "prep",
        prep_kernel,
        [((S, H), f32), ((K, ROW), f32), ((F, 3 * K), bf16), ((CUT, H), bf16)],
        (rank, cotangent, vt, cb, up_weight, out_weight),
        [SMEM, VMEM, VMEM, VMEM, HBM, HBM],
        [pltpu.VMEM((H, NF * D), bf16), pltpu.VMEM((S, 2 * NF, D), f32), dma((2,))],
        flops=2 * S * H * NF * D,
        nbytes=2 * (H * NF * D + CUT * H),
        limit=LARGE,
    )
    gain = ln_gain.reshape(1, FK)
    c6, wh, sc = call(
        "mlp",
        mlp_kernel,
        [((TP, S, FK + NF * DW), bf16), ((S, FK), f32), ((S, 128), f32)],
        (g6, gain, dh, up_lo, up_weight, out_weight),
        [VMEM, VMEM, VMEM, VMEM, HBM, HBM],
        [pltpu.VMEM((FK - CUT, H), bf16), pltpu.VMEM((H, NF * D), bf16), dma((2,))],
        limit=LARGE,
    )
    c6 = exchange(c6, "tensor")
    z, fm = call(
        "grad",
        grad_kernel,
        [((F, ROW), bf16), ((S, NF * DW), f32)],
        (c6, gain, wh, sc, x, cb, v, cotl, hot),
    )
    back = exchange(z.reshape(DP, 2, ROW), "dp").reshape(F, ROW)
    grad_t = call(
        "unpool",
        unpool_kernel,
        [((2, DW, samples), bf16)],
        (back, len_t),
        None,
        [pltpu.VMEM((F, ROW), f32), pltpu.VMEM((2, samples, DW), f32)],
    )
    layer_out = jnp.concatenate([fm.reshape(S, NF, DW).astype(bf16), lin], axis=1)
    return (layer_out, jnp.transpose(grad_t, (2, 0, 1)))


def solution(mesh):
    return jax.shard_map(
        shards,
        mesh=mesh,
        in_specs=(
            P(None, "dp", "tensor"),
            P(None, "dp"),
            P(),
            P(),
            P(),
            P(None, "tensor"),
            P("tensor", None),
            P(),
            P("dp", None, None),
        ),
        out_specs=(P("dp", None, "tensor"), P(None, "dp", "tensor")),
        check_vma=False,
    )
```

time: 97.2 us -> 91.8 us (0.944)
  blocking collectives: 36 us -> 13.6 us
  waiting for transfers between devices: 13.2 us -> 23.7 us
  starting transfers between devices: 27.4 us -> 37.2 us
  local copies, waits for them, and re-layouts: 10.6 us -> 2.9 us
  Pallas kernels: 7.31 us -> 12.6 us
    all_to_all x2 -> x1, blocking collectives: 36 us -> 13.6 us  [exchange(): return lax.all_to_all(x, axis, split_axis=0, concat_axis=0, tiled=True)]
    all_to_all x2 -> x3, waiting for transfers between devices: 13.2 us -> 23.7 us  [exchange(): return lax.all_to_all(x, axis, split_axis=0, concat_axis=0, tiled=True)]
    all_to_all x2 -> x3, starting transfers between devices: 27.4 us -> 37.2 us  [exchange(): return lax.all_to_all(x, axis, split_axis=0, concat_axis=0, tiled=True)]
    unnamed x22 -> x12, local copies, waits for them, and re-layouts: 8.53 us -> 2.81 us
    pallas_call x6 -> x7, Pallas kernels: 7.31 us -> 12.6 us  [call(): pl.pallas_call(kernel, out_shape=shapes if many else shapes[0], in_specs=...]
  transfers between devices with their start and end apart: 2 -> 3, of which waited for: 2 -> 3; matrix products, arithmetic and copies ran while one was open for 4% -> 1% of each run, Pallas kernels for 1% -> 4%
where the time goes in v2:
time: 91.8 us; the launch traced here: 91.3 us
  starting transfers between devices  37.2 us (41%)
  waiting for transfers between devices  23.7 us (26%)
  blocking collectives  13.6 us (15%)
  Pallas kernels  12.6 us (14%)
  local copies, waits for them, and re-layouts  2.9 us (3%)
    all_to_all x3, starting transfers between devices, exchange(): return lax.all_to_all(x, axis, split_axis=0, concat_axis=0, tiled=True)  37.2 us
    all_to_all x3, waiting for transfers between devices, exchange(): return lax.all_to_all(x, axis, split_axis=0, concat_axis=0, tiled=True)  23.7 us
    all_to_all x1, blocking collectives, exchange(): return lax.all_to_all(x, axis, split_axis=0, concat_axis=0, tiled=True)  13.6 us
    pallas_call x7, Pallas kernels, call(): pl.pallas_call(kernel, out_shape=shapes if many else shapes[0], in_specs=...  12.6 us
    unnamed x12, local copies, waits for them, and re-layouts  2.81 us
  transfers between devices with their start and end apart: 3, of which 3 were waited for; matrix products, arithmetic and copies ran while one was open for 1% of the time, Pallas kernels for 4%

profile of v2, /device:TPU:1, one launch (start us, length us, event | category | flops | bytes accessed | tf_op | source)
XLA Modules:
  0.0 91.3 jit_solution(14638772577215937669)
XLA Ops:
  0.6 1.8 %pool.1 = bf16[256,128]{1,0:T(8,128)(2,1)} custom-call(bf16[2,32,512]{2,1,0:T(8,128)(2,1)} %bitcast.22, s32[2,512]{1,0:T(2,128)} %bitcast.16), custom_call_target="tpu_custom_call" | custom-call | tf_op jit(solution)/shard_map/pool/pallas_call | solution.py:220
  2.5 17.8 %all-to-all-start = ((bf16[128,2,128]{2,1,0:T(2,128)(2,1)}), bf16[128,2,128]{2,1,0:T(2,128)(2,1)S(1)}, u32[]{:S(2)}, u32[]{:S(2)}) async-start(bf16[128,2,128]{2,1,0:T(2,128)(2,1)} %bitcast.21), calls=%async_computation | async-start | bytes 131072 | tf_op jit(solution)/shard_map/all_to_all | solution.py:235
  20.3 0.0 copy-start.3
  20.3 0.7 copy-done.3
  21.0 0.0 copy-start.4
  21.0 0.7 copy-done.4
  21.6 0.0 copy-start.5
  21.6 0.7 copy-done.5
  22.3 0.2 slots.1
  22.5 8.4 %all-to-all-done = bf16[128,2,128]{2,1,0:T(2,128)(2,1)S(1)} async-done(((bf16[128,2,128]{2,1,0:T(2,128)(2,1)}), bf16[128,2,128]{2,1,0:T(2,128)(2,1)S(1)}, u32[]{:S(2)}, u32[]{:S(2)}) %all-to-all-start) | async-done | bytes 65568 | tf_op jit(solution)/shard_map/all_to_all | solution.py:235
  30.9 1.0 %gram.1 = (bf16[6,32,256]{2,1,0:T(8,128)(2,1)}, bf16[256,128]{1,0:T(8,128)(2,1)S(1)}, bf16[64,128]{1,0:T(8,128)(2,1)S(1)}, bf16[4,8,32]{2,1,0:T(8,128)(2,1)S(1)}) custom-call(bf16[256,128]{1,0:T(8,128)(2,1)S(1)} %bitcast.12, bf16[16,256]{1,0:T(8,128)(2,1)S(1)} %get-tuple-element.17.vt_ref, bf16[256,256]{1,0:T(8,128)(2,1)S(1)} %get-tuple-element.18.hot_ref), custom_call_target="tpu_custom_call" | custom-call | tf_op jit(solution)/shard_map/gram/pallas_call | solution.py:220
  32.0 13.3 %all-to-all-start.1 = ((bf16[6,32,256]{2,1,0:T(8,128)(2,1)}), bf16[6,32,256]{2,1,0:T(8,128)(2,1)S(1)}, u32[]{:S(2)}, u32[]{:S(2)}) async-start(bf16[6,32,256]{2,1,0:T(8,128)(2,1)} %get-tuple-element.19), calls=%async_computation.1 | async-start | bytes 196608 | tf_op jit(solution)/shard_map/all_to_all | solution.py:235
  45.3 0.0 copy-start
  45.3 0.8 copy-done
  46.0 0.0 copy-start.1
  46.0 3.2 %prep.1 = (f32[4,1024]{1,0:T(4,128)S(1)}, f32[8,128]{1,0:T(8,128)S(1)}, bf16[256,24]{1,0:T(8,128)(2,1)S(1)}, bf16[1024,1024]{1,0:T(8,128)(2,1)S(1)}) custom-call(s32[1]{0:T(128)} %bitcast.8.rank_ref, bf16[4,16,192]{2,1,0:T(8,128)(2,1)S(1)} %copy-done, bf16[16,256]{1,0:T(8,128)(2,1)S(1)} %get-tuple-element.17.vt_ref, ...), custom_call_target="tpu_custom_call" | custom-call | flops 12582912 | bytes 5242880 | tf_op jit(solution)/shard_map/prep/pallas_call | solution.py:220
  49.3 5.3 %all-to-all-done.1.g_ref = bf16[6,32,256]{2,1,0:T(8,128)(2,1)S(1)} async-done(((bf16[6,32,256]{2,1,0:T(8,128)(2,1)}), bf16[6,32,256]{2,1,0:T(8,128)(2,1)S(1)}, u32[]{:S(2)}, u32[]{:S(2)}) %all-to-all-start.1) | async-done | bytes 98336 | tf_op jit(solution)/shard_map/all_to_all | solution.py:235
  54.6 0.0 copy-done.1
  54.6 0.0 copy-start.2
  54.6 4.0 %mlp.1 = (bf16[6,4,2304]{2,1,0:T(4,128)(2,1)S(1)}, f32[4,2048]{1,0:T(4,128)S(1)}, f32[4,128]{1,0:T(4,128)S(1)}) custom-call(bf16[6,32,256]{2,1,0:T(8,128)(2,1)S(1)} %all-to-all-done.1.g_ref, f32[1,2048]{1,0:T(1,128)S(1)} %bitcast.14, f32[4,1024]{1,0:T(4,128)S(1)} %get-tuple-element.21.dh_ref, bf16[1024,1024]{1,0:T(8,128)(2,1)S(1)} %get-tuple-element.22.lo_ref, ...), custom_call_target="tpu_custom_call" | custom-call | tf_op jit(solution)/shard_map/mlp/pallas_call | solution.py:220
  58.5 13.6 %all_to_all.20.c_ref = bf16[6,4,2304]{2,1,0:T(4,128)(2,1)S(1)} all-to-all(bf16[6,4,2304]{2,1,0:T(4,128)(2,1)S(1)} %get-tuple-element.23), channel_id=1, replica_groups=mesh['dp'=128,'tensor'=6] {'tensor'}, dimensions={0} | all-to-all | bytes 221184 | tf_op jit(solution)/shard_map/all_to_all | solution.py:235
  72.1 1.5 %grad.1 = (bf16[256,128]{1,0:T(8,128)(2,1)}, f32[4,256]{1,0:T(4,128)S(1)}) custom-call(bf16[6,4,2304]{2,1,0:T(4,128)(2,1)S(1)} %all_to_all.20.c_ref, f32[1,2048]{1,0:T(1,128)S(1)} %bitcast.15, f32[4,2048]{1,0:T(4,128)S(1)} %get-tuple-element.24.wh_ref, f32[4,128]{1,0:T(4,128)S(1)} %get-tuple-element.25.sc_ref, bf16[256,128]{1,0:T(8,128)(2,1)S(1)} %get-tuple-element.26.x_ref, ...), custom_call_target="tpu_custom_call" | custom-call | tf_op jit(solution)/shard_map/grad/pallas_call | solution.py:220
  73.6 6.1 %all-to-all-start.3 = ((bf16[128,2,128]{2,1,0:T(2,128)(2,1)}), bf16[128,2,128]{2,1,0:T(2,128)(2,1)S(1)}, u32[]{:S(2)}, u32[]{:S(2)}) async-start(bf16[128,2,128]{2,1,0:T(2,128)(2,1)} %bitcast.9), calls=%async_computation.3 | async-start | bytes 131072 | tf_op jit(solution)/shard_map/all_to_all | solution.py:235
  79.8 0.1 convert_element_type.7
  79.9 0.6 pad_maximum_fusion
  80.5 10.0 %all-to-all-done.3 = bf16[128,2,128]{2,1,0:T(2,128)(2,1)S(1)} async-done(((bf16[128,2,128]{2,1,0:T(2,128)(2,1)}), bf16[128,2,128]{2,1,0:T(2,128)(2,1)S(1)}, u32[]{:S(2)}, u32[]{:S(2)}) %all-to-all-start.3) | async-done | bytes 65568 | tf_op jit(solution)/shard_map/all_to_all | solution.py:235
  90.5 0.0 copy-done.2
  90.5 0.9 unpool.1
  (1 shorter events, 0.0 us)
Async XLA Ops:
  2.5 28.5 %all-to-all-start = ((bf16[128,2,128]{2,1,0:T(2,128)(2,1)}), bf16[128,2,128]{2,1,0:T(2,128)(2,1)S(1)}, u32[]{:S(2)}, u32[]{:S(2)}) async-start(bf16[128,2,128]{2,1,0:T(2,128)(2,1)} %bitcast.21), calls=%async_computation | async-start | bytes 131072 | tf_op jit(solution)/shard_map/all_to_all | solution.py:235
  20.3 0.7 copy-start.3
  21.0 0.7 copy-start.4
  21.6 0.7 copy-start.5
  32.0 22.6 %all-to-all-start.1 = ((bf16[6,32,256]{2,1,0:T(8,128)(2,1)}), bf16[6,32,256]{2,1,0:T(8,128)(2,1)S(1)}, u32[]{:S(2)}, u32[]{:S(2)}) async-start(bf16[6,32,256]{2,1,0:T(8,128)(2,1)} %get-tuple-element.19), calls=%async_computation.1 | async-start | bytes 196608 | tf_op jit(solution)/shard_map/all_to_all | solution.py:235
  45.3 0.8 copy-start
  46.0 8.5 %copy-start.1 = (f32[2048]{0:T(1024)S(1)}, f32[2048]{0:T(1024)}, u32[]{:S(2)}) copy-start(f32[2048]{0:T(1024)} %param.13) | copy-start | bytes 24580
  54.6 35.9 %copy-start.2 = (s32[512,2]{0,1:T(2,128)S(1)}, s32[512,2]{0,1:T(2,128)}, u32[]{:S(2)}) copy-start(s32[512,2]{0,1:T(2,128)} %param.10) | copy-start | bytes 12292
  73.6 16.8 %all-to-all-start.3 = ((bf16[128,2,128]{2,1,0:T(2,128)(2,1)}), bf16[128,2,128]{2,1,0:T(2,128)(2,1)S(1)}, u32[]{:S(2)}, u32[]{:S(2)}) async-start(bf16[128,2,128]{2,1,0:T(2,128)(2,1)} %bitcast.9), calls=%async_computation.3 | async-start | bytes 131072 | tf_op jit(solution)/shard_map/all_to_all | solution.py:235

commit v3 on v2

--- a/solution.py
+++ b/solution.py
@@ -18,6 +18,7 @@
 ROW = DW * S
 LARGE = 53_000_000
 WHOLE = 66_600_000
+PIECES = 4
 CUT = 1024
 bf16 = jnp.bfloat16
 f32 = jnp.float32
@@ -83,13 +84,6 @@
     out_ref[...] = pairs[...].astype(bf16)
 
 
-def slot_kernel(slot_ref, fm_ref, lc_ref, hot_ref, vt_ref):
-    onehot = jnp.where(slot_ref[...] == iota((F, F), 0), 1.0, 0.0).astype(bf16)
-    hot_ref[...] = onehot
-    both = rows([fm_ref[...].astype(f32), lc_ref[...].astype(f32)]).astype(bf16)
-    vt_ref[...] = dot_nt(both, onehot).astype(bf16)
-
-
 def gram_kernel(x_ref, vt_ref, hot_ref, g_ref, x_out, cb_ref, lin_ref):
     x = x_ref[...]
     x_out[...] = x
@@ -107,16 +101,31 @@
 
 
 def prep_kernel(
-    rank_ref, cot_ref, vt_ref, after_ref, up_hbm, ow_hbm, dh_ref, cotl_ref, v_ref, up_out, ow_ref, cot_scr, sem
+    rank_ref, slot_ref, fm_ref, lc_ref, cot_ref, up_hbm, ow_hbm,
+    hot_ref, vt_ref, dh_ref, cotl_ref, v_ref, up_out, ow_ref, cot_scr, sem,
 ):
-    ow_copy = pltpu.make_async_copy(ow_hbm, ow_ref, sem.at[0])
-    up_copy = pltpu.make_async_copy(up_hbm.at[pl.ds(0, CUT)], up_out, sem.at[1])
-    ow_copy.start()
-    up_copy.start()
-    cot_scr[...] = cot_ref[...].astype(f32)
-    vt = vt_ref[...].astype(f32)
+    step = H // PIECES
+    ow_copies = [
+        pltpu.make_async_copy(ow_hbm.at[pl.ds(p * step, step)], ow_ref.at[pl.ds(p * step, step)], sem.at[p])
+        for p in range(PIECES)
+    ]
+    step_up = CUT // PIECES
+    up_copies = [
+        pltpu.make_async_copy(
+            up_hbm.at[pl.ds(p * step_up, step_up)], up_out.at[pl.ds(p * step_up, step_up)], sem.at[PIECES + p]
+        )
+        for p in range(PIECES)
+    ]
+    for copy in ow_copies + up_copies:
+        copy.start()
+    onehot = jnp.where(slot_ref[...] == iota((F, F), 0), 1.0, 0.0).astype(bf16)
+    hot_ref[...] = onehot
+    both = rows([fm_ref[...].astype(f32), lc_ref[...].astype(f32)]).astype(bf16)
+    vt = dot_nt(both, onehot)
+    vt_ref[...] = vt.astype(bf16)
     v = vt.T
     v_ref[...] = lanes([v[:, :K], v]).astype(bf16)
+    cot_scr[...] = cot_ref[...].astype(f32)
     rank = rank_ref[0]
     parts = []
     for s in range(S):
@@ -127,16 +136,31 @@
         parts.append(own)
     cotl_ref[...] = lanes(parts)
     cot_fm = lanes([cot_scr[:, n, :] for n in range(NF)]).astype(bf16)
-    ow_copy.wait()
-    dh_ref[...] = dot_nt(cot_fm, ow_ref[...])
-    up_copy.wait()
+    for p in range(PIECES):
+        ow_copies[p].wait()
+        part = pl.ds(p * step, step)
+        dh_ref[:, part] = dot_nt(cot_fm, ow_ref[part, :])
+    for copy in up_copies:
+        copy.wait()
 
 
 def mlp_kernel(g_ref, gain_ref, dh_ref, lo_ref, up_hbm, ow_hbm, c_ref, wh_ref, sc_ref, hi_ref, ow_ref, sem):
-    up_copy = pltpu.make_async_copy(up_hbm.at[pl.ds(CUT, FK - CUT)], hi_ref, sem.at[0])
-    ow_copy = pltpu.make_async_copy(ow_hbm, ow_ref, sem.at[1])
-    up_copy.start()
-    ow_copy.start()
+    step_up = (FK - CUT) // PIECES
+    up_copies = [
+        pltpu.make_async_copy(
+            up_hbm.at[pl.ds(CUT + p * step_up, step_up)], hi_ref.at[pl.ds(p * step_up, step_up)], sem.at[p]
+        )
+        for p in range(PIECES)
+    ]
+    step = H // PIECES
+    ow_copies = [
+        pltpu.make_async_copy(
+            ow_hbm.at[pl.ds(p * step, step)], ow_ref.at[pl.ds(p * step, step)], sem.at[PIECES + p]
+        )
+        for p in range(PIECES)
+    ]
+    for copy in up_copies + ow_copies:
+        copy.start()
     g = g_ref[0].astype(f32)
     for t in range(1, TP):
         g = g + g_ref[t].astype(f32)
@@ -153,14 +177,16 @@
     sc_ref[...] = jnp.broadcast_to(scale, sc_ref.shape)
     normed = (whitened * gain_ref[...]).astype(bf16)
     up = dot(normed[:, :CUT], lo_ref[...])
-    up_copy.wait()
+    for copy in up_copies:
+        copy.wait()
     up = up + dot(normed[:, CUT:], hi_ref[...])
     sig = jax.nn.sigmoid(up)
     hidden = (up * sig).astype(bf16)
     d_up = (dh_ref[...] * (sig + up * sig * (1.0 - sig))).astype(bf16)
     d_lo = dot_nt(d_up, lo_ref[...]).astype(bf16)
     d_hi = dot_nt(d_up, hi_ref[...]).astype(bf16)
-    ow_copy.wait()
+    for copy in ow_copies:
+        copy.wait()
     fm = dot(hidden, ow_ref[...])
     for t in range(TP):
         c_ref[t, :, :CUT] = d_lo
@@ -170,11 +196,16 @@
         ).astype(bf16)
 
 
-def grad_kernel(c_ref, gain_ref, wh_ref, sc_ref, x_ref, cb_ref, v_ref, cotl_ref, hot_ref, z_ref, fm_ref):
+def grad_kernel(c_ref, gain_ref, wh_ref, sc_ref, x_ref, cb_ref, v_ref, cotl_ref, hot_ref, lin_ref, z_ref, layer_hbm, layer_scr, layer_ref, sem):
     c = c_ref[0].astype(f32)
     for t in range(1, TP):
         c = c + c_ref[t].astype(f32)
-    fm_ref[...] = c[:, FK:]
+    for n in range(NF):
+        layer_scr[:, n, :] = c[:, FK + n * DW : FK + (n + 1) * DW]
+    layer_scr[:, NF:, :] = lin_ref[...].astype(f32)
+    layer_ref[...] = layer_scr[...].astype(bf16)
+    layer_copy = pltpu.make_async_copy(layer_ref, layer_hbm, sem)
+    layer_copy.start()
     wh = wh_ref[...]
     gb = c[:, :FK] * gain_ref[...]
     flat = sc_ref[:, :1] * (
@@ -203,6 +234,7 @@
     dgt = dg.T.astype(bf16)
     left = lanes([dgt, dgt[:, :32], v_ref[...]])
     z_ref[...] = dot(left, right).astype(bf16)
+    layer_copy.wait()
 
 
 def unpool_kernel(z_ref, len_ref, out_ref, pairs, scr):
@@ -214,14 +246,14 @@
         out_ref[j] = (scr[j].T / len_ref[j : j + 1, :].astype(f32)).astype(bf16)
 
 
-def call(name, kernel, outs, args, specs=None, scratch=(), flops=0, nbytes=0, limit=16 * 2**20):
+def call(name, kernel, outs, args, specs=None, scratch=(), flops=0, nbytes=0, limit=16 * 2**20, out_specs=None):
     many = len(outs) > 1
     shapes = [jax.ShapeDtypeStruct(s, d) for s, d in outs]
     return pl.pallas_call(
         kernel,
         out_shape=shapes if many else shapes[0],
         in_specs=specs or [VMEM] * len(args),
-        out_specs=[VMEM] * len(outs) if many else VMEM,
+        out_specs=out_specs or ([VMEM] * len(outs) if many else VMEM),
         scratch_shapes=list(scratch),
         compiler_params=pltpu.CompilerParams(vmem_limit_bytes=limit),
         name=name,
@@ -266,11 +298,24 @@
         limit=WHOLE,
     )
     arrived = exchange(pooled.reshape(DP, 2, ROW), "dp").reshape(F, ROW)
-    hot, vt = call(
-        "slots",
-        slot_kernel,
-        [((F, F), bf16), ((2 * K, F), bf16)],
-        (feature_slot.reshape(1, F), fm_project.T, lc_weight.T),
+    rank = lax.axis_index("tensor").astype(jnp.int32).reshape(1)
+    hot, vt, dh, cotl, v, up_lo = call(
+        "prep",
+        prep_kernel,
+        [
+            ((F, F), bf16),
+            ((2 * K, F), bf16),
+            ((S, H), f32),
+            ((K, ROW), f32),
+            ((F, 3 * K), bf16),
+            ((CUT, H), bf16),
+        ],
+        (rank, feature_slot.reshape(1, F), fm_project.T, lc_weight.T, cotangent, up_weight, out_weight),
+        [SMEM, VMEM, VMEM, VMEM, VMEM, HBM, HBM],
+        [pltpu.VMEM((H, NF * D), bf16), pltpu.VMEM((S, 2 * NF, D), f32), dma((2 * PIECES,))],
+        flops=2 * S * H * NF * D,
+        nbytes=2 * (H * NF * D + CUT * H),
+        limit=LARGE,
     )
     g6, x, cb, lin = call(
         "gram",
@@ -279,18 +324,6 @@
         (arrived, vt, hot),
     )
     g6 = exchange(g6, "tensor")
-    rank = lax.axis_index("tensor").astype(jnp.int32).reshape(1)
-    dh, cotl, v, up_lo = call(
-        "prep",
-        prep_kernel,
-        [((S, H), f32), ((K, ROW), f32), ((F, 3 * K), bf16), ((CUT, H), bf16)],
-        (rank, cotangent, vt, cb, up_weight, out_weight),
-        [SMEM, VMEM, VMEM, VMEM, HBM, HBM],
-        [pltpu.VMEM((H, NF * D), bf16), pltpu.VMEM((S, 2 * NF, D), f32), dma((2,))],
-        flops=2 * S * H * NF * D,
-        nbytes=2 * (H * NF * D + CUT * H),
-        limit=LARGE,
-    )
     gain = ln_gain.reshape(1, FK)
     c6, wh, sc = call(
         "mlp",
@@ -298,15 +331,18 @@
         [((TP, S, FK + NF * DW), bf16), ((S, FK), f32), ((S, 128), f32)],
         (g6, gain, dh, up_lo, up_weight, out_weight),
         [VMEM, VMEM, VMEM, VMEM, HBM, HBM],
-        [pltpu.VMEM((FK - CUT, H), bf16), pltpu.VMEM((H, NF * D), bf16), dma((2,))],
+        [pltpu.VMEM((FK - CUT, H), bf16), pltpu.VMEM((H, NF * D), bf16), dma((2 * PIECES,))],
         limit=LARGE,
     )
     c6 = exchange(c6, "tensor")
-    z, fm = call(
+    z, layer_out = call(
         "grad",
         grad_kernel,
-        [((F, ROW), bf16), ((S, NF * DW), f32)],
-        (c6, gain, wh, sc, x, cb, v, cotl, hot),
+        [((F, ROW), bf16), ((S, 2 * NF, DW), bf16)],
+        (c6, gain, wh, sc, x, cb, v, cotl, hot, lin),
+        None,
+        [pltpu.VMEM((S, 2 * NF, DW), f32), pltpu.VMEM((S, 2 * NF, DW), bf16), dma],
+        out_specs=[VMEM, HBM],
     )
     back = exchange(z.reshape(DP, 2, ROW), "dp").reshape(F, ROW)
     grad_t = call(
@@ -317,7 +353,6 @@
         None,
         [pltpu.VMEM((F, ROW), f32), pltpu.VMEM((2, samples, DW), f32)],
     )
-    layer_out = jnp.concatenate([fm.reshape(S, NF, DW).astype(bf16), lin], axis=1)
     return (layer_out, jnp.transpose(grad_t, (2, 0, 1)))
 
 

time: 91.8 us -> 93.1 us (1.014)
  blocking collectives: 13.6 us -> 55 us
  starting transfers between devices: 37.2 us -> 17.8 us
  waiting for transfers between devices: 23.7 us -> 4.35 us
    all_to_all x1 -> x3, blocking collectives: 13.6 us -> 55 us  [exchange(): return lax.all_to_all(x, axis, split_axis=0, concat_axis=0, tiled=True)]
    all_to_all x3 -> x1, starting transfers between devices: 37.2 us -> 17.8 us  [exchange(): return lax.all_to_all(x, axis, split_axis=0, concat_axis=0, tiled=True)]
    all_to_all x3 -> x1, waiting for transfers between devices: 23.7 us -> 4.35 us  [exchange(): return lax.all_to_all(x, axis, split_axis=0, concat_axis=0, tiled=True)]
    pallas_call x7 -> x6, Pallas kernels: 12.6 us -> 11.9 us  [call(): pl.pallas_call(kernel, out_shape=shapes if many else shapes[0], in_specs=...]
  transfers between devices with their start and end apart: 3 -> 1, of which waited for: 3 -> 1; matrix products, arithmetic and copies ran while one was open for 1% -> 0% of each run, Pallas kernels for 4% -> 4%
where the time goes in v3:
time: 93.1 us; the launch traced here: 92.6 us
  blocking collectives  55 us (59%)
  starting transfers between devices  17.8 us (19%)
  Pallas kernels  11.9 us (13%)
  waiting for transfers between devices  4.35 us (5%)
  local copies, waits for them, and re-layouts  2.81 us (3%)
    all_to_all x3, blocking collectives, exchange(): return lax.all_to_all(x, axis, split_axis=0, concat_axis=0, tiled=True)  55 us
    all_to_all x1, starting transfers between devices, exchange(): return lax.all_to_all(x, axis, split_axis=0, concat_axis=0, tiled=True)  17.8 us
    pallas_call x6, Pallas kernels, call(): pl.pallas_call(kernel, out_shape=shapes if many else shapes[0], in_specs=...  11.9 us
    all_to_all x1, waiting for transfers between devices, exchange(): return lax.all_to_all(x, axis, split_axis=0, concat_axis=0, tiled=True)  4.35 us
    unnamed x12, local copies, waits for them, and re-layouts  2.81 us
  transfers between devices with their start and end apart: 1, of which 1 were waited for; matrix products, arithmetic and copies ran while one was open for 0% of the time, Pallas kernels for 4%

profile of v3, /device:TPU:1, one launch (start us, length us, event | category | flops | bytes accessed | tf_op | source)
XLA Modules:
  0.0 92.6 jit_solution(3862431075377415084)
XLA Ops:
  0.6 1.8 %pool.1 = bf16[256,128]{1,0:T(8,128)(2,1)} custom-call(bf16[2,32,512]{2,1,0:T(8,128)(2,1)} %bitcast.23, s32[2,512]{1,0:T(2,128)} %bitcast.17), custom_call_target="tpu_custom_call" | custom-call | tf_op jit(solution)/shard_map/pool/pallas_call | solution.py:252
  2.5 17.8 %all-to-all-start = ((bf16[128,2,128]{2,1,0:T(2,128)(2,1)}), bf16[128,2,128]{2,1,0:T(2,128)(2,1)S(1)}, u32[]{:S(2)}, u32[]{:S(2)}) async-start(bf16[128,2,128]{2,1,0:T(2,128)(2,1)} %bitcast.22), calls=%async_computation | async-start | bytes 131072 | tf_op jit(solution)/shard_map/all_to_all | solution.py:267
  20.3 0.0 copy-start
  20.3 0.7 copy-done
  21.0 0.0 copy-start.3
  21.0 0.7 copy-done.3
  21.7 0.0 copy-start.4
  21.7 0.7 copy-done.4
  22.4 0.0 copy-start.5
  22.4 0.7 copy-done.5
  23.1 0.0 copy-start.1
  23.1 3.5 %prep.1 = (bf16[256,256]{1,0:T(8,128)(2,1)S(1)}, bf16[16,256]{1,0:T(8,128)(2,1)S(1)}, f32[4,1024]{1,0:T(4,128)S(1)}, f32[8,128]{1,0:T(8,128)S(1)}, bf16[256,24]{...) custom-call(s32[1]{0:T(128)} %bitcast.4.rank_ref, s32[1,256]{1,0:T(1,128)S(1)} %bitcast.21, bf16[8,256]{1,0:T(8,128)(2,1)S(1)} %bitcast.19, ...), custom_call_target="tpu_custom_call" | custom-call | flops 12582912 | bytes 5242880 | tf_op jit(solution)/shard_map/prep/pallas_call | solution.py:252
  26.6 4.4 %all-to-all-done = bf16[128,2,128]{2,1,0:T(2,128)(2,1)S(1)} async-done(((bf16[128,2,128]{2,1,0:T(2,128)(2,1)}), bf16[128,2,128]{2,1,0:T(2,128)(2,1)S(1)}, u32[]{:S(2)}, u32[]{:S(2)}) %all-to-all-start) | async-done | bytes 65568 | tf_op jit(solution)/shard_map/all_to_all | solution.py:267
  30.9 0.4 gram.1
  31.3 22.4 %all_to_all.20.g_ref = bf16[6,32,256]{2,1,0:T(8,128)(2,1)S(1)} all-to-all(bf16[6,32,256]{2,1,0:T(8,128)(2,1)S(1)} %get-tuple-element.19), channel_id=1, replica_groups=mesh['dp'=128,'tensor'=6] {'tensor'}, dimensions={0} | all-to-all | bytes 196608 | tf_op jit(solution)/shard_map/all_to_all | solution.py:267
  53.7 0.0 copy-done.1
  53.7 0.0 copy-start.2
  53.7 4.0 %mlp.1 = (bf16[6,4,2304]{2,1,0:T(4,128)(2,1)S(1)}, f32[4,2048]{1,0:T(4,128)S(1)}, f32[4,128]{1,0:T(4,128)S(1)}) custom-call(bf16[6,32,256]{2,1,0:T(8,128)(2,1)S(1)} %all_to_all.20.g_ref, f32[1,2048]{1,0:T(1,128)S(1)} %bitcast.15, f32[4,1024]{1,0:T(4,128)S(1)} %get-tuple-element.20.dh_ref, bf16[1024,1024]{1,0:T(8,128)(2,1)S(1)} %get-tuple-element.21.lo_ref, ...), custom_call_target="tpu_custom_call" | custom-call | tf_op jit(solution)/shard_map/mlp/pallas_call | solution.py:252
  57.7 13.6 %all_to_all.21.c_ref = bf16[6,4,2304]{2,1,0:T(4,128)(2,1)S(1)} all-to-all(bf16[6,4,2304]{2,1,0:T(4,128)(2,1)S(1)} %get-tuple-element.22), channel_id=1, replica_groups=mesh['dp'=128,'tensor'=6] {'tensor'}, dimensions={0} | all-to-all | bytes 221184 | tf_op jit(solution)/shard_map/all_to_all | solution.py:267
  71.3 1.4 %grad.1 = (bf16[256,128]{1,0:T(8,128)(2,1)S(1)}, bf16[4,16,32]{2,1,0:T(8,128)(2,1)}) custom-call(bf16[6,4,2304]{2,1,0:T(4,128)(2,1)S(1)} %all_to_all.21.c_ref, f32[1,2048]{1,0:T(1,128)S(1)} %bitcast.16, f32[4,2048]{1,0:T(4,128)S(1)} %get-tuple-element.23.wh_ref, f32[4,128]{1,0:T(4,128)S(1)} %get-tuple-element.24.sc_ref, ...), custom_call_target="tpu_custom_call" | custom-call | tf_op jit(solution)/shard_map/grad/pallas_call | solution.py:252
  72.7 19.1 %all_to_all.22 = bf16[128,2,128]{2,1,0:T(2,128)(2,1)S(1)} all-to-all(bf16[128,2,128]{2,1,0:T(2,128)(2,1)S(1)} %bitcast.14), channel_id=1, replica_groups=mesh['dp'=128,'tensor'=6] {'dp'}, dimensions={0} | all-to-all | bytes 131072 | tf_op jit(solution)/shard_map/all_to_all | solution.py:267
  91.7 0.0 copy-done.2
  91.7 0.9 unpool.1
Async XLA Ops:
  2.5 28.5 %all-to-all-start = ((bf16[128,2,128]{2,1,0:T(2,128)(2,1)}), bf16[128,2,128]{2,1,0:T(2,128)(2,1)S(1)}, u32[]{:S(2)}, u32[]{:S(2)}) async-start(bf16[128,2,128]{2,1,0:T(2,128)(2,1)} %bitcast.22), calls=%async_computation | async-start | bytes 131072 | tf_op jit(solution)/shard_map/all_to_all | solution.py:267
  20.3 0.8 copy-start
  21.0 0.7 copy-start.3
  21.7 0.7 copy-start.4
  22.4 0.7 copy-start.5
  23.1 30.6 %copy-start.1 = (f32[2048]{0:T(1024)S(1)}, f32[2048]{0:T(1024)}, u32[]{:S(2)}) copy-start(f32[2048]{0:T(1024)} %param.13) | copy-start | bytes 24580
  53.7 38.0 %copy-start.2 = (s32[512,2]{0,1:T(2,128)S(1)}, s32[512,2]{0,1:T(2,128)}, u32[]{:S(2)}) copy-start(s32[512,2]{0,1:T(2,128)} %param.10) | copy-start | bytes 12292

commit v4 on v3

--- a/solution.py
+++ b/solution.py
@@ -12,6 +12,8 @@
 S = 4
 DW = 32
 TP = 6
+TENSOR = ("z_hi", "core")
+PEERS = ("core", "z_hi")
 DP = 128
 H = 1024
 FK = F * K
@@ -19,7 +21,7 @@
 LARGE = 53_000_000
 WHOLE = 66_600_000
 PIECES = 4
-CUT = 1024
+CUT = 1280
 bf16 = jnp.bfloat16
 f32 = jnp.float32
 
@@ -92,9 +94,11 @@
         lin_ref[s] = y[K:, s * DW : (s + 1) * DW].astype(bf16)
     hi, lo = split(jnp.where(own_sample(), rows([y[:K]] * S), 0.0))
     cb = rows([hi, lo])
-    cb_ref[...] = cb
+    cb_ref[...] = hi
     g = dot_nt(cb, x)
-    g = (g[:32] + g[32:]).astype(bf16)
+    g = (g[:32] + g[32:]).reshape(S, K, F)
+    mean = jnp.sum(jnp.sum(g, axis=2, keepdims=True), axis=1, keepdims=True) / FK
+    g = (g - mean).reshape(S * K, F).astype(bf16)
     g = dot(g, hot_ref[...]).astype(bf16)
     for t in range(TP):
         g_ref[t] = g
@@ -124,7 +128,7 @@
     vt = dot_nt(both, onehot)
     vt_ref[...] = vt.astype(bf16)
     v = vt.T
-    v_ref[...] = lanes([v[:, :K], v]).astype(bf16)
+    v_ref[...] = v.astype(bf16)
     cot_scr[...] = cot_ref[...].astype(f32)
     rank = rank_ref[0]
     parts = []
@@ -145,17 +149,18 @@
 
 
 def mlp_kernel(g_ref, gain_ref, dh_ref, lo_ref, up_hbm, ow_hbm, c_ref, wh_ref, sc_ref, hi_ref, ow_ref, sem):
-    step_up = (FK - CUT) // PIECES
+    step_up = 256
+    up_pieces = (FK - CUT) // step_up
     up_copies = [
         pltpu.make_async_copy(
             up_hbm.at[pl.ds(CUT + p * step_up, step_up)], hi_ref.at[pl.ds(p * step_up, step_up)], sem.at[p]
         )
-        for p in range(PIECES)
+        for p in range(up_pieces)
     ]
     step = H // PIECES
     ow_copies = [
         pltpu.make_async_copy(
-            ow_hbm.at[pl.ds(p * step, step)], ow_ref.at[pl.ds(p * step, step)], sem.at[PIECES + p]
+            ow_hbm.at[pl.ds(p * step, step)], ow_ref.at[pl.ds(p * step, step)], sem.at[up_pieces + p]
         )
         for p in range(PIECES)
     ]
@@ -165,9 +170,7 @@
     for t in range(1, TP):
         g = g + g_ref[t].astype(f32)
     g = rows([g[:, c * 32 : (c + 1) * 32] for c in range(8)])
-    hi, lo = split(g)
-    m = dot(rows([hi, lo]), expander())
-    m = jnp.where(own_rank(), m[:256] + m[256:], 0.0)
+    m = jnp.where(own_rank(), dot(g.astype(bf16), expander()), 0.0)
     m = jnp.sum(m.reshape(8 * S, K, 256), axis=1)
     flat = lanes([m[c * S : (c + 1) * S] for c in range(8)])
     centered = flat - jnp.mean(flat, axis=1, keepdims=True)
@@ -177,35 +180,33 @@
     sc_ref[...] = jnp.broadcast_to(scale, sc_ref.shape)
     normed = (whitened * gain_ref[...]).astype(bf16)
     up = dot(normed[:, :CUT], lo_ref[...])
-    for copy in up_copies:
-        copy.wait()
-    up = up + dot(normed[:, CUT:], hi_ref[...])
+    for p in range(up_pieces):
+        up_copies[p].wait()
+        part = slice(p * step_up, (p + 1) * step_up)
+        up = up + dot(normed[:, CUT + p * step_up : CUT + (p + 1) * step_up], hi_ref[part, :])
     sig = jax.nn.sigmoid(up)
     hidden = (up * sig).astype(bf16)
     d_up = (dh_ref[...] * (sig + up * sig * (1.0 - sig))).astype(bf16)
     d_lo = dot_nt(d_up, lo_ref[...]).astype(bf16)
     d_hi = dot_nt(d_up, hi_ref[...]).astype(bf16)
-    for copy in ow_copies:
-        copy.wait()
-    fm = dot(hidden, ow_ref[...])
-    for t in range(TP):
-        c_ref[t, :, :CUT] = d_lo
-        c_ref[t, :, CUT:FK] = d_hi
-        c_ref[t, :, FK:] = lanes(
+    fm = jnp.zeros((S, NF * D), f32)
+    for p in range(PIECES):
+        ow_copies[p].wait()
+        fm = fm + dot(hidden[:, p * step : (p + 1) * step], ow_ref[p * step : (p + 1) * step, :])
+    for q in range(TP):
+        t = (q % 3) * 2 + q // 3
+        c_ref[q, :, :CUT] = d_lo
+        c_ref[q, :, CUT:FK] = d_hi
+        c_ref[q, :, FK:] = lanes(
             [fm[:, n * D + t * DW : n * D + (t + 1) * DW] for n in range(NF)]
         ).astype(bf16)
 
 
-def grad_kernel(c_ref, gain_ref, wh_ref, sc_ref, x_ref, cb_ref, v_ref, cotl_ref, hot_ref, lin_ref, z_ref, layer_hbm, layer_scr, layer_ref, sem):
+def grad_kernel(c_ref, gain_ref, wh_ref, sc_ref, x_ref, cb_ref, v_ref, cotl_ref, hot_ref, z_ref, fm_ref):
     c = c_ref[0].astype(f32)
     for t in range(1, TP):
         c = c + c_ref[t].astype(f32)
-    for n in range(NF):
-        layer_scr[:, n, :] = c[:, FK + n * DW : FK + (n + 1) * DW]
-    layer_scr[:, NF:, :] = lin_ref[...].astype(f32)
-    layer_ref[...] = layer_scr[...].astype(bf16)
-    layer_copy = pltpu.make_async_copy(layer_ref, layer_hbm, sem)
-    layer_copy.start()
+    fm_ref[...] = c[:, FK:]
     wh = wh_ref[...]
     gb = c[:, :FK] * gain_ref[...]
     flat = sc_ref[:, :1] * (
@@ -219,22 +220,14 @@
             for c in range(8)
         ]
     )
-    hi, lo = split(jnp.where(own_rank(), spread, 0.0))
-    dg = dot_nt(rows([hi, lo]), expander())
-    dg = dg[:256] + dg[256:]
-    dg = lanes([dg[c * 32 : (c + 1) * 32] for c in range(8)])
-    hi, lo = split(dg)
-    dg = dot_nt(rows([hi, lo]), hot_ref[...])
-    dc = dot(dg.astype(bf16), x_ref[...])
-    dc = jnp.where(own_sample(), dc[:32] + dc[32:], 0.0)
+    dg = dot_nt(jnp.where(own_rank(), spread, 0.0).astype(bf16), expander())
+    dg = lanes([dg[c * 32 : (c + 1) * 32] for c in range(8)]).astype(bf16)
+    dg = dot_nt(dg, hot_ref[...])
+    dc = jnp.where(own_sample(), dot(dg.astype(bf16), x_ref[...]), 0.0)
     dc = jnp.sum(dc.reshape(S, K, ROW), axis=0)
-    dc_hi = dc.astype(bf16).astype(f32)
-    cb = cb_ref[...].astype(f32)
-    right = rows([cb[:32], cb[:32], cb[32:], dc_hi, dc - dc_hi, cotl_ref[...]]).astype(bf16)
-    dgt = dg.T.astype(bf16)
-    left = lanes([dgt, dgt[:, :32], v_ref[...]])
+    right = rows([cb_ref[...].astype(f32), dc, cotl_ref[...]]).astype(bf16)
+    left = lanes([dg.T.astype(bf16), v_ref[...]])
     z_ref[...] = dot(left, right).astype(bf16)
-    layer_copy.wait()
 
 
 def unpool_kernel(z_ref, len_ref, out_ref, pairs, scr):
@@ -246,14 +239,14 @@
         out_ref[j] = (scr[j].T / len_ref[j : j + 1, :].astype(f32)).astype(bf16)
 
 
-def call(name, kernel, outs, args, specs=None, scratch=(), flops=0, nbytes=0, limit=16 * 2**20, out_specs=None):
+def call(name, kernel, outs, args, specs=None, scratch=(), flops=0, nbytes=0, limit=16 * 2**20):
     many = len(outs) > 1
     shapes = [jax.ShapeDtypeStruct(s, d) for s, d in outs]
     return pl.pallas_call(
         kernel,
         out_shape=shapes if many else shapes[0],
         in_specs=specs or [VMEM] * len(args),
-        out_specs=out_specs or ([VMEM] * len(outs) if many else VMEM),
+        out_specs=[VMEM] * len(outs) if many else VMEM,
         scratch_shapes=list(scratch),
         compiler_params=pltpu.CompilerParams(vmem_limit_bytes=limit),
         name=name,
@@ -298,7 +291,7 @@
         limit=WHOLE,
     )
     arrived = exchange(pooled.reshape(DP, 2, ROW), "dp").reshape(F, ROW)
-    rank = lax.axis_index("tensor").astype(jnp.int32).reshape(1)
+    rank = lax.axis_index(TENSOR).astype(jnp.int32).reshape(1)
     hot, vt, dh, cotl, v, up_lo = call(
         "prep",
         prep_kernel,
@@ -307,7 +300,7 @@
             ((2 * K, F), bf16),
             ((S, H), f32),
             ((K, ROW), f32),
-            ((F, 3 * K), bf16),
+            ((F, 2 * K), bf16),
             ((CUT, H), bf16),
         ],
         (rank, feature_slot.reshape(1, F), fm_project.T, lc_weight.T, cotangent, up_weight, out_weight),
@@ -320,10 +313,10 @@
     g6, x, cb, lin = call(
         "gram",
         gram_kernel,
-        [((TP, S * K, F), bf16), ((F, ROW), bf16), ((2 * S * K, ROW), bf16), ((S, K, DW), bf16)],
+        [((TP, S * K, F), bf16), ((F, ROW), bf16), ((S * K, ROW), bf16), ((S, K, DW), bf16)],
         (arrived, vt, hot),
     )
-    g6 = exchange(g6, "tensor")
+    g6 = exchange(g6, PEERS)
     gain = ln_gain.reshape(1, FK)
     c6, wh, sc = call(
         "mlp",
@@ -334,15 +327,12 @@
         [pltpu.VMEM((FK - CUT, H), bf16), pltpu.VMEM((H, NF * D), bf16), dma((2 * PIECES,))],
         limit=LARGE,
     )
-    c6 = exchange(c6, "tensor")
-    z, layer_out = call(
+    c6 = exchange(c6, PEERS)
+    z, fm = call(
         "grad",
         grad_kernel,
-        [((F, ROW), bf16), ((S, 2 * NF, DW), bf16)],
-        (c6, gain, wh, sc, x, cb, v, cotl, hot, lin),
-        None,
-        [pltpu.VMEM((S, 2 * NF, DW), f32), pltpu.VMEM((S, 2 * NF, DW), bf16), dma],
-        out_specs=[VMEM, HBM],
+        [((F, ROW), bf16), ((S, NF * DW), f32)],
+        (c6, gain, wh, sc, x, cb, v, cotl, hot),
     )
     back = exchange(z.reshape(DP, 2, ROW), "dp").reshape(F, ROW)
     grad_t = call(
@@ -353,24 +343,26 @@
         None,
         [pltpu.VMEM((F, ROW), f32), pltpu.VMEM((2, samples, DW), f32)],
     )
+    layer_out = jnp.concatenate([fm.reshape(S, NF, DW).astype(bf16), lin], axis=1)
     return (layer_out, jnp.transpose(grad_t, (2, 0, 1)))
 
 
 def solution(mesh):
+    parts = jax.sharding.Mesh(mesh.devices.reshape(DP, 3, 2), ("dp",) + TENSOR)
     return jax.shard_map(
         shards,
-        mesh=mesh,
+        mesh=parts,
         in_specs=(
-            P(None, "dp", "tensor"),
+            P(None, "dp", TENSOR),
             P(None, "dp"),
             P(),
             P(),
             P(),
-            P(None, "tensor"),
-            P("tensor", None),
+            P(None, TENSOR),
+            P(TENSOR, None),
             P(),
             P("dp", None, None),
         ),
-        out_specs=(P("dp", None, "tensor"), P(None, "dp", "tensor")),
+        out_specs=(P("dp", None, TENSOR), P(None, "dp", TENSOR)),
         check_vma=False,
     )

time: 93.1 us -> 93.8 us (level)
  blocking collectives: 55 us -> 36 us
  waiting for transfers between devices: 4.35 us -> 14.1 us
  starting transfers between devices: 17.8 us -> 26.5 us
    all_to_all x3 -> x2, blocking collectives: 55 us -> 36 us  [exchange(): return lax.all_to_all(x, axis, split_axis=0, concat_axis=0, tiled=True)]
    all_to_all x1 -> x2, waiting for transfers between devices: 4.35 us -> 14.1 us  [exchange(): return lax.all_to_all(x, axis, split_axis=0, concat_axis=0, tiled=True)]
    all_to_all x1 -> x2, starting transfers between devices: 17.8 us -> 26.5 us  [exchange(): return lax.all_to_all(x, axis, split_axis=0, concat_axis=0, tiled=True)]
  transfers between devices with their start and end apart: 1 -> 2, of which waited for: 1 -> 2; matrix products, arithmetic and copies ran while one was open for 0% -> 1% of each run, Pallas kernels for 4% -> 4%
where the time goes in v4:
time: 93.8 us; the launch traced here: 93.3 us
  blocking collectives  36 us (38%)
  starting transfers between devices  26.5 us (28%)
  waiting for transfers between devices  14.1 us (15%)
  Pallas kernels  12.5 us (13%)
  local copies, waits for them, and re-layouts  2.9 us (3%)
    all_to_all x2, blocking collectives, exchange(): return lax.all_to_all(x, axis, split_axis=0, concat_axis=0, tiled=True)  36 us
    all_to_all x2, starting transfers between devices, exchange(): return lax.all_to_all(x, axis, split_axis=0, concat_axis=0, tiled=True)  26.5 us
    all_to_all x2, waiting for transfers between devices, exchange(): return lax.all_to_all(x, axis, split_axis=0, concat_axis=0, tiled=True)  14.1 us
    pallas_call x6, Pallas kernels, call(): pl.pallas_call(kernel, out_shape=shapes if many else shapes[0], in_specs=...  12.5 us
    unnamed x12, local copies, waits for them, and re-layouts  2.81 us
  transfers between devices with their start and end apart: 2, of which 2 were waited for; matrix products, arithmetic and copies ran while one was open for 1% of the time, Pallas kernels for 4%

profile of v4, /device:TPU:1, one launch (start us, length us, event | category | flops | bytes accessed | tf_op | source)
XLA Modules:
  0.0 93.3 jit_solution(4860995835509408491)
XLA Ops:
  0.6 1.8 %pool.1 = bf16[256,128]{1,0:T(8,128)(2,1)} custom-call(bf16[2,32,512]{2,1,0:T(8,128)(2,1)} %bitcast.22, s32[2,512]{1,0:T(2,128)} %bitcast.16), custom_call_target="tpu_custom_call" | custom-call | tf_op jit(solution)/shard_map/pool/pallas_call | solution.py:245
  2.5 17.8 %all-to-all-start = ((bf16[128,2,128]{2,1,0:T(2,128)(2,1)}), bf16[128,2,128]{2,1,0:T(2,128)(2,1)S(1)}, u32[]{:S(2)}, u32[]{:S(2)}) async-start(bf16[128,2,128]{2,1,0:T(2,128)(2,1)} %bitcast.21), calls=%async_computation | async-start | bytes 131072 | tf_op jit(solution)/shard_map/all_to_all | solution.py:260
  20.3 0.0 copy-start
  20.3 0.7 copy-done
  21.0 0.0 copy-start.3
  21.0 0.7 copy-done.3
  21.7 0.0 copy-start.4
  21.7 0.7 copy-done.4
  22.4 0.0 copy-start.5
  22.4 0.7 copy-done.5
  23.1 0.0 copy-start.1
  23.1 3.6 %prep.1 = (bf16[256,256]{1,0:T(8,128)(2,1)S(1)}, bf16[16,256]{1,0:T(8,128)(2,1)S(1)}, f32[4,1024]{1,0:T(4,128)S(1)}, f32[8,128]{1,0:T(8,128)S(1)}, bf16[256,16]{...) custom-call(s32[1]{0:T(128)} %bitcast.4.rank_ref, s32[1,256]{1,0:T(1,128)S(1)} %bitcast.20, bf16[8,256]{1,0:T(8,128)(2,1)S(1)} %bitcast.18, ...), custom_call_target="tpu_custom_call" | custom-call | flops 12582912 | bytes 5767168 | tf_op jit(solution)/shard_map/prep/pallas_call | solution.py:245
  26.8 4.2 %all-to-all-done = bf16[128,2,128]{2,1,0:T(2,128)(2,1)S(1)} async-done(((bf16[128,2,128]{2,1,0:T(2,128)(2,1)}), bf16[128,2,128]{2,1,0:T(2,128)(2,1)S(1)}, u32[]{:S(2)}, u32[]{:S(2)}) %all-to-all-start) | async-done | bytes 65568 | tf_op jit(solution)/shard_map/all_to_all | solution.py:260
  30.9 0.5 gram.1
  31.4 22.4 %all_to_all.20.g_ref = bf16[6,32,256]{2,1,0:T(8,128)(2,1)S(1)} all-to-all(bf16[6,32,256]{2,1,0:T(8,128)(2,1)S(1)} %get-tuple-element.19), channel_id=1, replica_groups=mesh['dp'=128,'z_hi'=3,'core'=2] {'core','z_hi'}, dimensions={0} | all-to-all | bytes 196608 | tf_op jit(solution)/shard_map/all_to_all | solution.py:260
  53.8 0.0 copy-done.1
  53.8 0.0 copy-start.2
  53.8 4.3 %mlp.1 = (bf16[6,4,2304]{2,1,0:T(4,128)(2,1)S(1)}, f32[4,2048]{1,0:T(4,128)S(1)}, f32[4,128]{1,0:T(4,128)S(1)}) custom-call(bf16[6,32,256]{2,1,0:T(8,128)(2,1)S(1)} %all_to_all.20.g_ref, f32[1,2048]{1,0:T(1,128)S(1)} %bitcast.14, f32[4,1024]{1,0:T(4,128)S(1)} %get-tuple-element.20.dh_ref, bf16[1280,1024]{1,0:T(8,128)(2,1)S(1)} %get-tuple-element.21.lo_ref, ...), custom_call_target="tpu_custom_call" | custom-call | tf_op jit(solution)/shard_map/mlp/pallas_call | solution.py:245
  58.1 13.6 %all_to_all.21.c_ref = bf16[6,4,2304]{2,1,0:T(4,128)(2,1)S(1)} all-to-all(bf16[6,4,2304]{2,1,0:T(4,128)(2,1)S(1)} %get-tuple-element.22), channel_id=1, replica_groups=mesh['dp'=128,'z_hi'=3,'core'=2] {'core','z_hi'}, dimensions={0} | all-to-all | bytes 221184 | tf_op jit(solution)/shard_map/all_to_all | solution.py:260
  71.7 1.4 %grad.1 = (bf16[256,128]{1,0:T(8,128)(2,1)}, f32[4,256]{1,0:T(4,128)S(1)}) custom-call(bf16[6,4,2304]{2,1,0:T(4,128)(2,1)S(1)} %all_to_all.21.c_ref, f32[1,2048]{1,0:T(1,128)S(1)} %bitcast.15, f32[4,2048]{1,0:T(4,128)S(1)} %get-tuple-element.23.wh_ref, f32[4,128]{1,0:T(4,128)S(1)} %get-tuple-element.24.sc_ref, bf16[256,128]{1,0:T(8,128)(2,1)S(1)} %get-tuple-element.25.x_ref, ...), custom_call_target="tpu_custom_call" | custom-call | tf_op jit(solution)/shard_map/grad/pallas_call | solution.py:245
  73.1 8.7 %all-to-all-start.3 = ((bf16[128,2,128]{2,1,0:T(2,128)(2,1)}), bf16[128,2,128]{2,1,0:T(2,128)(2,1)S(1)}, u32[]{:S(2)}, u32[]{:S(2)}) async-start(bf16[128,2,128]{2,1,0:T(2,128)(2,1)} %bitcast.9), calls=%async_computation.3 | async-start | bytes 131072 | tf_op jit(solution)/shard_map/all_to_all | solution.py:260
  81.8 0.1 convert_element_type.7
  81.8 0.6 pad_maximum_fusion
  82.5 10.0 %all-to-all-done.3 = bf16[128,2,128]{2,1,0:T(2,128)(2,1)S(1)} async-done(((bf16[128,2,128]{2,1,0:T(2,128)(2,1)}), bf16[128,2,128]{2,1,0:T(2,128)(2,1)S(1)}, u32[]{:S(2)}, u32[]{:S(2)}) %all-to-all-start.3) | async-done | bytes 65568 | tf_op jit(solution)/shard_map/all_to_all | solution.py:260
  92.4 0.0 copy-done.2
  92.4 0.9 unpool.1
  (1 shorter events, 0.0 us)
Async XLA Ops:
  2.5 28.5 %all-to-all-start = ((bf16[128,2,128]{2,1,0:T(2,128)(2,1)}), bf16[128,2,128]{2,1,0:T(2,128)(2,1)S(1)}, u32[]{:S(2)}, u32[]{:S(2)}) async-start(bf16[128,2,128]{2,1,0:T(2,128)(2,1)} %bitcast.21), calls=%async_computation | async-start | bytes 131072 | tf_op jit(solution)/shard_map/all_to_all | solution.py:260
  20.3 0.8 copy-start
  21.0 0.7 copy-start.3
  21.7 0.7 copy-start.4
  22.4 0.7 copy-start.5
  23.1 30.7 %copy-start.1 = (f32[2048]{0:T(1024)S(1)}, f32[2048]{0:T(1024)}, u32[]{:S(2)}) copy-start(f32[2048]{0:T(1024)} %param.13) | copy-start | bytes 24580
  53.8 38.6 %copy-start.2 = (s32[512,2]{0,1:T(2,128)S(1)}, s32[512,2]{0,1:T(2,128)}, u32[]{:S(2)}) copy-start(s32[512,2]{0,1:T(2,128)} %param.10) | copy-start | bytes 12292
  73.1 19.4 %all-to-all-start.3 = ((bf16[128,2,128]{2,1,0:T(2,128)(2,1)}), bf16[128,2,128]{2,1,0:T(2,128)(2,1)S(1)}, u32[]{:S(2)}, u32[]{:S(2)}) async-start(bf16[128,2,128]{2,1,0:T(2,128)(2,1)} %bitcast.9), calls=%async_computation.3 | async-start | bytes 131072 | tf_op jit(solution)/shard_map/all_to_all | solution.py:260

commit v5 on v2

--- a/solution.py
+++ b/solution.py
@@ -13,6 +13,9 @@
 DW = 32
 TP = 6
 DP = 128
+TURN = 79
+DP_ORDER = [(q + TURN) % DP for q in range(DP)]
+PEERS = [4, 0, 2, 5, 1, 3]
 H = 1024
 FK = F * K
 ROW = DW * S
@@ -80,11 +83,12 @@
         pairs[pl.ds(j, DP, stride=2), :] = lanes(
             [scr[j, pl.ds(s, DP, stride=S), :] for s in range(S)]
         )
-    out_ref[...] = pairs[...].astype(bf16)
+    turned = rows([pairs[2 * TURN :, :], pairs[: 2 * TURN, :]]) if TURN else pairs[...]
+    out_ref[...] = turned.astype(bf16)
 
 
 def slot_kernel(slot_ref, fm_ref, lc_ref, hot_ref, vt_ref):
-    onehot = jnp.where(slot_ref[...] == iota((F, F), 0), 1.0, 0.0).astype(bf16)
+    onehot = jnp.where(slot_ref[...] == (iota((F, F), 0) + 2 * TURN) % F, 1.0, 0.0).astype(bf16)
     hot_ref[...] = onehot
     both = rows([fm_ref[...].astype(f32), lc_ref[...].astype(f32)]).astype(bf16)
     vt_ref[...] = dot_nt(both, onehot).astype(bf16)
@@ -162,10 +166,11 @@
     d_hi = dot_nt(d_up, hi_ref[...]).astype(bf16)
     ow_copy.wait()
     fm = dot(hidden, ow_ref[...])
-    for t in range(TP):
-        c_ref[t, :, :CUT] = d_lo
-        c_ref[t, :, CUT:FK] = d_hi
-        c_ref[t, :, FK:] = lanes(
+    for q in range(TP):
+        t = PEERS[q]
+        c_ref[q, :, :CUT] = d_lo
+        c_ref[q, :, CUT:FK] = d_hi
+        c_ref[q, :, FK:] = lanes(
             [fm[:, n * D + t * DW : n * D + (t + 1) * DW] for n in range(NF)]
         ).astype(bf16)
 
@@ -206,7 +211,8 @@
 
 
 def unpool_kernel(z_ref, len_ref, out_ref, pairs, scr):
-    pairs[...] = z_ref[...].astype(f32)
+    z = z_ref[...].astype(f32)
+    pairs[...] = rows([z[F - 2 * TURN :], z[: F - 2 * TURN]]) if TURN else z
     for j in range(2):
         z = pairs[pl.ds(j, DP, stride=2), :]
         for s in range(S):
@@ -231,8 +237,8 @@
     )(*args)
 
 
-def exchange(x, axis):
-    return lax.all_to_all(x, axis, split_axis=0, concat_axis=0, tiled=True)
+def exchange(x, axis, order):
+    return lax.all_to_all(x, axis, split_axis=0, concat_axis=0, axis_index_groups=[order], tiled=True)
 
 
 def shards(
@@ -265,7 +271,7 @@
         ],
         limit=WHOLE,
     )
-    arrived = exchange(pooled.reshape(DP, 2, ROW), "dp").reshape(F, ROW)
+    arrived = exchange(pooled.reshape(DP, 2, ROW), "dp", DP_ORDER).reshape(F, ROW)
     hot, vt = call(
         "slots",
         slot_kernel,
@@ -278,7 +284,7 @@
         [((TP, S * K, F), bf16), ((F, ROW), bf16), ((2 * S * K, ROW), bf16), ((S, K, DW), bf16)],
         (arrived, vt, hot),
     )
-    g6 = exchange(g6, "tensor")
+    g6 = exchange(g6, "tensor", PEERS)
     rank = lax.axis_index("tensor").astype(jnp.int32).reshape(1)
     dh, cotl, v, up_lo = call(
         "prep",
@@ -301,14 +307,14 @@
         [pltpu.VMEM((FK - CUT, H), bf16), pltpu.VMEM((H, NF * D), bf16), dma((2,))],
         limit=LARGE,
     )
-    c6 = exchange(c6, "tensor")
+    c6 = exchange(c6, "tensor", PEERS)
     z, fm = call(
         "grad",
         grad_kernel,
         [((F, ROW), bf16), ((S, NF * DW), f32)],
         (c6, gain, wh, sc, x, cb, v, cotl, hot),
     )
-    back = exchange(z.reshape(DP, 2, ROW), "dp").reshape(F, ROW)
+    back = exchange(z.reshape(DP, 2, ROW), "dp", DP_ORDER).reshape(F, ROW)
     grad_t = call(
         "unpool",
         unpool_kernel,

time: 91.8 us -> 82.2 us (0.90)
  waiting for transfers between devices: 23.7 us -> 3.27 us
  starting transfers between devices: 37.2 us -> 47.5 us
    all_to_all x3, waiting for transfers between devices: 23.7 us -> 3.27 us  [exchange(): lax.all_to_all(x, axis, split_axis=0, concat_axis=0, axis_index_groups=[o...]
    all_to_all x3, starting transfers between devices: 37.2 us -> 47.5 us  [exchange(): lax.all_to_all(x, axis, split_axis=0, concat_axis=0, axis_index_groups=[o...]
where the time goes in v5:
time: 82.2 us; the launch traced here: 81.7 us
  starting transfers between devices  47.5 us (58%)
  blocking collectives  14 us (17%)
  Pallas kernels  12.6 us (15%)
  waiting for transfers between devices  3.27 us (4%)
  local copies, waits for them, and re-layouts  2.9 us (4%)
    all_to_all x3, starting transfers between devices, exchange(): lax.all_to_all(x, axis, split_axis=0, concat_axis=0, axis_index_groups=[o...  47.5 us
    all_to_all x1, blocking collectives, exchange(): lax.all_to_all(x, axis, split_axis=0, concat_axis=0, axis_index_groups=[o...  14 us
    pallas_call x7, Pallas kernels, call(): pl.pallas_call(kernel, out_shape=shapes if many else shapes[0], in_specs=...  12.6 us
    all_to_all x3, waiting for transfers between devices, exchange(): lax.all_to_all(x, axis, split_axis=0, concat_axis=0, axis_index_groups=[o...  3.27 us
    unnamed x12, local copies, waits for them, and re-layouts  2.81 us
  transfers between devices with their start and end apart: 3, of which 3 were waited for; matrix products, arithmetic and copies ran while one was open for 1% of the time, Pallas kernels for 4%

profile of v5, /device:TPU:1, one launch (start us, length us, event | category | flops | bytes accessed | tf_op | source)
XLA Modules:
  0.0 81.7 jit_solution(8781470191852266520)
XLA Ops:
  0.6 1.8 %pool.1 = bf16[256,128]{1,0:T(8,128)(2,1)} custom-call(bf16[2,32,512]{2,1,0:T(8,128)(2,1)} %bitcast.22, s32[2,512]{1,0:T(2,128)} %bitcast.16), custom_call_target="tpu_custom_call" | custom-call | tf_op jit(solution)/shard_map/pool/pallas_call | solution.py:226
  2.5 19.5 %all-to-all-start = ((bf16[128,2,128]{2,1,0:T(2,128)(2,1)}), bf16[128,2,128]{2,1,0:T(2,128)(2,1)S(1)}, u32[]{:S(2)}, u32[]{:S(2)}) async-start(bf16[128,2,128]{2,1,0:T(2,128)(2,1)} %bitcast.21), calls=%async_computation | async-start | bytes 131072 | tf_op jit(solution)/shard_map/all_to_all | solution.py:241
  22.0 0.0 copy-start.3
  22.0 0.7 copy-done.3
  22.7 0.0 copy-start.4
  22.7 0.7 copy-done.4
  23.3 0.0 copy-start.5
  23.3 0.7 copy-done.5
  24.0 0.2 slots.1
  24.2 0.4 all-to-all-done
  24.6 1.0 %gram.1 = (bf16[6,32,256]{2,1,0:T(8,128)(2,1)}, bf16[256,128]{1,0:T(8,128)(2,1)S(1)}, bf16[64,128]{1,0:T(8,128)(2,1)S(1)}, bf16[4,8,32]{2,1,0:T(8,128)(2,1)S(1)}) custom-call(bf16[256,128]{1,0:T(8,128)(2,1)S(1)} %bitcast.12, bf16[16,256]{1,0:T(8,128)(2,1)S(1)} %get-tuple-element.17.vt_ref, bf16[256,256]{1,0:T(8,128)(2,1)S(1)} %get-tuple-element.18.hot_ref), custom_call_target="tpu_custom_call" | custom-call | tf_op jit(solution)/shard_map/gram/pallas_call | solution.py:226
  25.7 14.7 %all-to-all-start.1 = ((bf16[6,32,256]{2,1,0:T(8,128)(2,1)}), bf16[6,32,256]{2,1,0:T(8,128)(2,1)S(1)}, u32[]{:S(2)}, u32[]{:S(2)}) async-start(bf16[6,32,256]{2,1,0:T(8,128)(2,1)} %get-tuple-element.19), calls=%async_computation.1 | async-start | bytes 196608 | tf_op jit(solution)/shard_map/all_to_all | solution.py:241
  40.4 0.0 copy-start
  40.4 0.8 copy-done
  41.1 0.0 copy-start.1
  41.1 3.2 %prep.1 = (f32[4,1024]{1,0:T(4,128)S(1)}, f32[8,128]{1,0:T(8,128)S(1)}, bf16[256,24]{1,0:T(8,128)(2,1)S(1)}, bf16[1024,1024]{1,0:T(8,128)(2,1)S(1)}) custom-call(s32[1]{0:T(128)} %bitcast.8.rank_ref, bf16[4,16,192]{2,1,0:T(8,128)(2,1)S(1)} %copy-done, bf16[16,256]{1,0:T(8,128)(2,1)S(1)} %get-tuple-element.17.vt_ref, ...), custom_call_target="tpu_custom_call" | custom-call | flops 12582912 | bytes 5242880 | tf_op jit(solution)/shard_map/prep/pallas_call | solution.py:226
  44.4 0.9 %all-to-all-done.1.g_ref = bf16[6,32,256]{2,1,0:T(8,128)(2,1)S(1)} async-done(((bf16[6,32,256]{2,1,0:T(8,128)(2,1)}), bf16[6,32,256]{2,1,0:T(8,128)(2,1)S(1)}, u32[]{:S(2)}, u32[]{:S(2)}) %all-to-all-start.1) | async-done | bytes 98336 | tf_op jit(solution)/shard_map/all_to_all | solution.py:241
  45.2 0.0 copy-done.1
  45.2 0.0 copy-start.2
  45.2 4.0 %mlp.1 = (bf16[6,4,2304]{2,1,0:T(4,128)(2,1)S(1)}, f32[4,2048]{1,0:T(4,128)S(1)}, f32[4,128]{1,0:T(4,128)S(1)}) custom-call(bf16[6,32,256]{2,1,0:T(8,128)(2,1)S(1)} %all-to-all-done.1.g_ref, f32[1,2048]{1,0:T(1,128)S(1)} %bitcast.14, f32[4,1024]{1,0:T(4,128)S(1)} %get-tuple-element.21.dh_ref, bf16[1024,1024]{1,0:T(8,128)(2,1)S(1)} %get-tuple-element.22.lo_ref, ...), custom_call_target="tpu_custom_call" | custom-call | tf_op jit(solution)/shard_map/mlp/pallas_call | solution.py:226
  49.2 14.0 %all_to_all.20.c_ref = bf16[6,4,2304]{2,1,0:T(4,128)(2,1)S(1)} all-to-all(bf16[6,4,2304]{2,1,0:T(4,128)(2,1)S(1)} %get-tuple-element.23), channel_id=1, replica_groups={{4,0,2,5,1,3},{10,6,8,11,7,9},{16,12,14,17,13,15},{22,18,20,23,19,21},{..., dimensions={0} | all-to-all | bytes 221184 | tf_op jit(solution)/shard_map/all_to_all | solution.py:241
  63.3 1.5 %grad.1 = (bf16[256,128]{1,0:T(8,128)(2,1)}, f32[4,256]{1,0:T(4,128)S(1)}) custom-call(bf16[6,4,2304]{2,1,0:T(4,128)(2,1)S(1)} %all_to_all.20.c_ref, f32[1,2048]{1,0:T(1,128)S(1)} %bitcast.15, f32[4,2048]{1,0:T(4,128)S(1)} %get-tuple-element.24.wh_ref, f32[4,128]{1,0:T(4,128)S(1)} %get-tuple-element.25.sc_ref, bf16[256,128]{1,0:T(8,128)(2,1)S(1)} %get-tuple-element.26.x_ref, ...), custom_call_target="tpu_custom_call" | custom-call | tf_op jit(solution)/shard_map/grad/pallas_call | solution.py:226
  64.8 13.3 %all-to-all-start.3 = ((bf16[128,2,128]{2,1,0:T(2,128)(2,1)}), bf16[128,2,128]{2,1,0:T(2,128)(2,1)S(1)}, u32[]{:S(2)}, u32[]{:S(2)}) async-start(bf16[128,2,128]{2,1,0:T(2,128)(2,1)} %bitcast.9), calls=%async_computation.3 | async-start | bytes 131072 | tf_op jit(solution)/shard_map/all_to_all | solution.py:241
  78.1 0.1 convert_element_type.7
  78.2 0.6 pad_maximum_fusion
  78.8 2.0 %all-to-all-done.3 = bf16[128,2,128]{2,1,0:T(2,128)(2,1)S(1)} async-done(((bf16[128,2,128]{2,1,0:T(2,128)(2,1)}), bf16[128,2,128]{2,1,0:T(2,128)(2,1)S(1)}, u32[]{:S(2)}, u32[]{:S(2)}) %all-to-all-start.3) | async-done | bytes 65568 | tf_op jit(solution)/shard_map/all_to_all | solution.py:241
  80.8 0.0 copy-done.2
  80.8 0.9 %unpool.1 = bf16[2,32,512]{2,1,0:T(8,128)(2,1)} custom-call(bf16[256,128]{1,0:T(8,128)(2,1)S(1)} %bitcast.13, s32[2,512]{1,0:T(2,128)S(1)} %bitcast.17), custom_call_target="tpu_custom_call" | custom-call | tf_op jit(solution)/shard_map/unpool/pallas_call | solution.py:226
  (1 shorter events, 0.0 us)
Async XLA Ops:
  2.5 22.2 %all-to-all-start = ((bf16[128,2,128]{2,1,0:T(2,128)(2,1)}), bf16[128,2,128]{2,1,0:T(2,128)(2,1)S(1)}, u32[]{:S(2)}, u32[]{:S(2)}) async-start(bf16[128,2,128]{2,1,0:T(2,128)(2,1)} %bitcast.21), calls=%async_computation | async-start | bytes 131072 | tf_op jit(solution)/shard_map/all_to_all | solution.py:241
  22.0 0.7 copy-start.3
  22.7 0.7 copy-start.4
  23.3 0.7 copy-start.5
  25.7 19.6 %all-to-all-start.1 = ((bf16[6,32,256]{2,1,0:T(8,128)(2,1)}), bf16[6,32,256]{2,1,0:T(8,128)(2,1)S(1)}, u32[]{:S(2)}, u32[]{:S(2)}) async-start(bf16[6,32,256]{2,1,0:T(8,128)(2,1)} %get-tuple-element.19), calls=%async_computation.1 | async-start | bytes 196608 | tf_op jit(solution)/shard_map/all_to_all | solution.py:241
  40.4 0.8 copy-start
  41.1 4.1 %copy-start.1 = (f32[2048]{0:T(1024)S(1)}, f32[2048]{0:T(1024)}, u32[]{:S(2)}) copy-start(f32[2048]{0:T(1024)} %param.13) | copy-start | bytes 24580
  45.2 35.5 %copy-start.2 = (s32[512,2]{0,1:T(2,128)S(1)}, s32[512,2]{0,1:T(2,128)}, u32[]{:S(2)}) copy-start(s32[512,2]{0,1:T(2,128)} %param.10) | copy-start | bytes 12292
  64.8 16.0 %all-to-all-start.3 = ((bf16[128,2,128]{2,1,0:T(2,128)(2,1)}), bf16[128,2,128]{2,1,0:T(2,128)(2,1)S(1)}, u32[]{:S(2)}, u32[]{:S(2)}) async-start(bf16[128,2,128]{2,1,0:T(2,128)(2,1)} %bitcast.9), calls=%async_computation.3 | async-start | bytes 131072 | tf_op jit(solution)/shard_map/all_to_all | solution.py:241

commit v6 on v5

--- a/solution.py
+++ b/solution.py
@@ -210,7 +210,11 @@
     z_ref[...] = dot(left, right).astype(bf16)
 
 
-def unpool_kernel(z_ref, len_ref, out_ref, pairs, scr):
+def unpool_kernel(z_ref, len_ref, fm_ref, lin_ref, out_ref, layer_ref, pairs, scr, layer):
+    for n in range(NF):
+        layer[:, n, :] = fm_ref[:, n * DW : (n + 1) * DW]
+    layer[:, NF:, :] = lin_ref[...].astype(f32)
+    layer_ref[...] = layer[...].astype(bf16)
     z = z_ref[...].astype(f32)
     pairs[...] = rows([z[F - 2 * TURN :], z[: F - 2 * TURN]]) if TURN else z
     for j in range(2):
@@ -315,15 +319,14 @@
         (c6, gain, wh, sc, x, cb, v, cotl, hot),
     )
     back = exchange(z.reshape(DP, 2, ROW), "dp", DP_ORDER).reshape(F, ROW)
-    grad_t = call(
+    grad_t, layer_out = call(
         "unpool",
         unpool_kernel,
-        [((2, DW, samples), bf16)],
-        (back, len_t),
+        [((2, DW, samples), bf16), ((S, 2 * NF, DW), bf16)],
+        (back, len_t, fm, lin),
         None,
-        [pltpu.VMEM((F, ROW), f32), pltpu.VMEM((2, samples, DW), f32)],
-    )
-    layer_out = jnp.concatenate([fm.reshape(S, NF, DW).astype(bf16), lin], axis=1)
+        [pltpu.VMEM((F, ROW), f32), pltpu.VMEM((2, samples, DW), f32), pltpu.VMEM((S, 2 * NF, DW), f32)],
+    )
     return (layer_out, jnp.transpose(grad_t, (2, 0, 1)))
 
 

time: 82.2 us -> 81.1 us (0.987)
  blocking collectives: 14 us -> 29.6 us
  starting transfers between devices: 47.5 us -> 34.2 us
  waiting for transfers between devices: 3.27 us -> 1.3 us
    all_to_all x1 -> x2, blocking collectives: 14 us -> 29.6 us  [exchange(): lax.all_to_all(x, axis, split_axis=0, concat_axis=0, axis_index_groups=[o...]
    all_to_all x3 -> x2, starting transfers between devices: 47.5 us -> 34.2 us  [exchange(): lax.all_to_all(x, axis, split_axis=0, concat_axis=0, axis_index_groups=[o...]
    all_to_all x3 -> x2, waiting for transfers between devices: 3.27 us -> 1.3 us  [exchange(): lax.all_to_all(x, axis, split_axis=0, concat_axis=0, axis_index_groups=[o...]
  transfers between devices with their start and end apart: 3 -> 2, of which waited for: 3 -> 2; matrix products, arithmetic and copies ran while one was open for 1% -> 0% of each run, Pallas kernels for 4% -> 4%
where the time goes in v6:
time: 81.1 us; the launch traced here: 80.6 us
  starting transfers between devices  34.2 us (42%)
  blocking collectives  29.6 us (36%)
  Pallas kernels  12 us (15%)
  local copies, waits for them, and re-layouts  2.81 us (3%)
  waiting for transfers between devices  1.3 us (2%)
    all_to_all x2, starting transfers between devices, exchange(): lax.all_to_all(x, axis, split_axis=0, concat_axis=0, axis_index_groups=[o...  34.2 us
    all_to_all x2, blocking collectives, exchange(): lax.all_to_all(x, axis, split_axis=0, concat_axis=0, axis_index_groups=[o...  29.6 us
    pallas_call x7, Pallas kernels, call(): pl.pallas_call(kernel, out_shape=shapes if many else shapes[0], in_specs=...  12 us
    unnamed x12, local copies, waits for them, and re-layouts  2.81 us
  transfers between devices with their start and end apart: 2, of which 2 were waited for; matrix products, arithmetic and copies ran while one was open for 0% of the time, Pallas kernels for 4%

profile of v6, /device:TPU:1, one launch (start us, length us, event | category | flops | bytes accessed | tf_op | source)
XLA Modules:
  0.0 80.6 jit_solution(17600352932204934197)
XLA Ops:
  0.6 1.8 %pool.1 = bf16[256,128]{1,0:T(8,128)(2,1)} custom-call(bf16[2,32,512]{2,1,0:T(8,128)(2,1)} %bitcast.23, s32[2,512]{1,0:T(2,128)} %bitcast.17), custom_call_target="tpu_custom_call" | custom-call | tf_op jit(solution)/shard_map/pool/pallas_call | solution.py:230
  2.5 19.5 %all-to-all-start = ((bf16[128,2,128]{2,1,0:T(2,128)(2,1)}), bf16[128,2,128]{2,1,0:T(2,128)(2,1)S(1)}, u32[]{:S(2)}, u32[]{:S(2)}) async-start(bf16[128,2,128]{2,1,0:T(2,128)(2,1)} %bitcast.22), calls=%async_computation | async-start | bytes 131072 | tf_op jit(solution)/shard_map/all_to_all | solution.py:245
  22.0 0.0 copy-start.3
  22.0 0.7 copy-done.3
  22.7 0.0 copy-start.4
  22.7 0.7 copy-done.4
  23.3 0.0 copy-start.5
  23.4 0.7 copy-done.5
  24.0 0.2 slots.1
  24.2 0.4 all-to-all-done
  24.6 1.0 %gram.1 = (bf16[6,32,256]{2,1,0:T(8,128)(2,1)}, bf16[256,128]{1,0:T(8,128)(2,1)S(1)}, bf16[64,128]{1,0:T(8,128)(2,1)S(1)}, bf16[4,8,32]{2,1,0:T(8,128)(2,1)S(1)}) custom-call(bf16[256,128]{1,0:T(8,128)(2,1)S(1)} %bitcast.12, bf16[16,256]{1,0:T(8,128)(2,1)S(1)} %get-tuple-element.19.vt_ref, bf16[256,256]{1,0:T(8,128)(2,1)S(1)} %get-tuple-element.20.hot_ref), custom_call_target="tpu_custom_call" | custom-call | tf_op jit(solution)/shard_map/gram/pallas_call | solution.py:230
  25.7 14.7 %all-to-all-start.1 = ((bf16[6,32,256]{2,1,0:T(8,128)(2,1)}), bf16[6,32,256]{2,1,0:T(8,128)(2,1)S(1)}, u32[]{:S(2)}, u32[]{:S(2)}) async-start(bf16[6,32,256]{2,1,0:T(8,128)(2,1)} %get-tuple-element.21), calls=%async_computation.1 | async-start | bytes 196608 | tf_op jit(solution)/shard_map/all_to_all | solution.py:245
  40.4 0.0 copy-start
  40.4 0.8 copy-done
  41.1 0.0 copy-start.1
  41.1 3.2 %prep.1 = (f32[4,1024]{1,0:T(4,128)S(1)}, f32[8,128]{1,0:T(8,128)S(1)}, bf16[256,24]{1,0:T(8,128)(2,1)S(1)}, bf16[1024,1024]{1,0:T(8,128)(2,1)S(1)}) custom-call(s32[1]{0:T(128)} %bitcast.8.rank_ref, bf16[4,16,192]{2,1,0:T(8,128)(2,1)S(1)} %copy-done, bf16[16,256]{1,0:T(8,128)(2,1)S(1)} %get-tuple-element.19.vt_ref, ...), custom_call_target="tpu_custom_call" | custom-call | flops 12582912 | bytes 5242880 | tf_op jit(solution)/shard_map/prep/pallas_call | solution.py:230
  44.4 0.9 %all-to-all-done.1.g_ref = bf16[6,32,256]{2,1,0:T(8,128)(2,1)S(1)} async-done(((bf16[6,32,256]{2,1,0:T(8,128)(2,1)}), bf16[6,32,256]{2,1,0:T(8,128)(2,1)S(1)}, u32[]{:S(2)}, u32[]{:S(2)}) %all-to-all-start.1) | async-done | bytes 98336 | tf_op jit(solution)/shard_map/all_to_all | solution.py:245
  45.2 0.0 copy-done.1
  45.2 0.0 copy-start.2
  45.2 4.0 %mlp.1 = (bf16[6,4,2304]{2,1,0:T(4,128)(2,1)S(1)}, f32[4,2048]{1,0:T(4,128)S(1)}, f32[4,128]{1,0:T(4,128)S(1)}) custom-call(bf16[6,32,256]{2,1,0:T(8,128)(2,1)S(1)} %all-to-all-done.1.g_ref, f32[1,2048]{1,0:T(1,128)S(1)} %bitcast.15, f32[4,1024]{1,0:T(4,128)S(1)} %get-tuple-element.23.dh_ref, bf16[1024,1024]{1,0:T(8,128)(2,1)S(1)} %get-tuple-element.24.lo_ref, ...), custom_call_target="tpu_custom_call" | custom-call | tf_op jit(solution)/shard_map/mlp/pallas_call | solution.py:230
  49.2 14.0 %all_to_all.20.c_ref = bf16[6,4,2304]{2,1,0:T(4,128)(2,1)S(1)} all-to-all(bf16[6,4,2304]{2,1,0:T(4,128)(2,1)S(1)} %get-tuple-element.25), channel_id=1, replica_groups={{4,0,2,5,1,3},{10,6,8,11,7,9},{16,12,14,17,13,15},{22,18,20,23,19,21},{..., dimensions={0} | all-to-all | bytes 221184 | tf_op jit(solution)/shard_map/all_to_all | solution.py:245
  63.3 0.9 %grad.1 = (bf16[256,128]{1,0:T(8,128)(2,1)S(1)}, f32[4,256]{1,0:T(4,128)S(1)}) custom-call(bf16[6,4,2304]{2,1,0:T(4,128)(2,1)S(1)} %all_to_all.20.c_ref, f32[1,2048]{1,0:T(1,128)S(1)} %bitcast.16, f32[4,2048]{1,0:T(4,128)S(1)} %get-tuple-element.26.wh_ref, f32[4,128]{1,0:T(4,128)S(1)} %get-tuple-element.27.sc_ref, ...), custom_call_target="tpu_custom_call" | custom-call | tf_op jit(solution)/shard_map/grad/pallas_call | solution.py:230
  64.1 15.6 %all_to_all.21 = bf16[128,2,128]{2,1,0:T(2,128)(2,1)S(1)} all-to-all(bf16[128,2,128]{2,1,0:T(2,128)(2,1)S(1)} %bitcast.14), channel_id=1, replica_groups={{474,480,486,492,498,504,510,516,522,528,534,540,546,552,558,564,570,57..., dimensions={0} | all-to-all | bytes 131072 | tf_op jit(solution)/shard_map/all_to_all | solution.py:245
  79.7 0.0 copy-done.2
  79.7 0.9 %unpool.1 = (bf16[2,32,512]{2,1,0:T(8,128)(2,1)}, bf16[4,16,32]{2,1,0:T(8,128)(2,1)}) custom-call(bf16[256,128]{1,0:T(8,128)(2,1)S(1)} %bitcast.13, s32[2,512]{1,0:T(2,128)S(1)} %bitcast.18, f32[4,256]{1,0:T(4,128)S(1)} %get-tuple-element.32.fm_ref, bf16[4,8,32]{2,1,0:T(8,128)(2,1)S(1)} %get-tuple-element.33.lin_ref), custom_call_target="tpu_custom_call" | custom-call | tf_op jit(solution)/shard_map/unpool/pallas_call | solution.py:230
Async XLA Ops:
  2.5 22.2 %all-to-all-start = ((bf16[128,2,128]{2,1,0:T(2,128)(2,1)}), bf16[128,2,128]{2,1,0:T(2,128)(2,1)S(1)}, u32[]{:S(2)}, u32[]{:S(2)}) async-start(bf16[128,2,128]{2,1,0:T(2,128)(2,1)} %bitcast.22), calls=%async_computation | async-start | bytes 131072 | tf_op jit(solution)/shard_map/all_to_all | solution.py:245
  22.0 0.7 copy-start.3
  22.7 0.7 copy-start.4
  23.3 0.7 copy-start.5
  25.7 19.6 %all-to-all-start.1 = ((bf16[6,32,256]{2,1,0:T(8,128)(2,1)}), bf16[6,32,256]{2,1,0:T(8,128)(2,1)S(1)}, u32[]{:S(2)}, u32[]{:S(2)}) async-start(bf16[6,32,256]{2,1,0:T(8,128)(2,1)} %get-tuple-element.21), calls=%async_computation.1 | async-start | bytes 196608 | tf_op jit(solution)/shard_map/all_to_all | solution.py:245
  40.4 0.8 copy-start
  41.1 4.1 %copy-start.1 = (f32[2048]{0:T(1024)S(1)}, f32[2048]{0:T(1024)}, u32[]{:S(2)}) copy-start(f32[2048]{0:T(1024)} %param.13) | copy-start | bytes 24580
  45.2 34.5 %copy-start.2 = (s32[512,2]{0,1:T(2,128)S(1)}, s32[512,2]{0,1:T(2,128)}, u32[]{:S(2)}) copy-start(s32[512,2]{0,1:T(2,128)} %param.10) | copy-start | bytes 12292

commit v7 on v6

--- a/solution.py
+++ b/solution.py
@@ -104,7 +104,9 @@
     cb = rows([hi, lo])
     cb_ref[...] = cb
     g = dot_nt(cb, x)
-    g = (g[:32] + g[32:]).astype(bf16)
+    g = (g[:32] + g[32:]).reshape(S, K, F)
+    mean = jnp.sum(jnp.sum(g, axis=2, keepdims=True), axis=1, keepdims=True) / FK
+    g = (g - mean).reshape(S * K, F).astype(bf16)
     g = dot(g, hot_ref[...]).astype(bf16)
     for t in range(TP):
         g_ref[t] = g

time: 81.1 us -> 81.2 us (level)
  no operation moved by 1% of the time
where the time goes in v7:
time: 81.2 us; the launch traced here: 80.7 us
  starting transfers between devices  34.2 us (42%)
  blocking collectives  29.6 us (36%)
  Pallas kernels  12.1 us (15%)
  local copies, waits for them, and re-layouts  2.81 us (3%)
  waiting for transfers between devices  1.3 us (2%)
    all_to_all x2, starting transfers between devices, exchange(): lax.all_to_all(x, axis, split_axis=0, concat_axis=0, axis_index_groups=[o...  34.2 us
    all_to_all x2, blocking collectives, exchange(): lax.all_to_all(x, axis, split_axis=0, concat_axis=0, axis_index_groups=[o...  29.6 us
    pallas_call x7, Pallas kernels, call(): pl.pallas_call(kernel, out_shape=shapes if many else shapes[0], in_specs=...  12.1 us
    unnamed x12, local copies, waits for them, and re-layouts  2.81 us
  transfers between devices with their start and end apart: 2, of which 2 were waited for; matrix products, arithmetic and copies ran while one was open for 0% of the time, Pallas kernels for 4%

profile of v7, /device:TPU:1, one launch (start us, length us, event | category | flops | bytes accessed | tf_op | source)
XLA Modules:
  0.0 80.7 jit_solution(16117789423859870073)
XLA Ops:
  0.6 1.8 %pool.1 = bf16[256,128]{1,0:T(8,128)(2,1)} custom-call(bf16[2,32,512]{2,1,0:T(8,128)(2,1)} %bitcast.23, s32[2,512]{1,0:T(2,128)} %bitcast.17), custom_call_target="tpu_custom_call" | custom-call | tf_op jit(solution)/shard_map/pool/pallas_call | solution.py:232
  2.5 19.5 %all-to-all-start = ((bf16[128,2,128]{2,1,0:T(2,128)(2,1)}), bf16[128,2,128]{2,1,0:T(2,128)(2,1)S(1)}, u32[]{:S(2)}, u32[]{:S(2)}) async-start(bf16[128,2,128]{2,1,0:T(2,128)(2,1)} %bitcast.22), calls=%async_computation | async-start | bytes 131072 | tf_op jit(solution)/shard_map/all_to_all | solution.py:247
  22.0 0.0 copy-start.3
  22.0 0.7 copy-done.3
  22.7 0.0 copy-start.4
  22.7 0.7 copy-done.4
  23.3 0.0 copy-start.5
  23.4 0.7 copy-done.5
  24.0 0.2 slots.1
  24.2 0.4 all-to-all-done
  24.6 1.1 %gram.1 = (bf16[6,32,256]{2,1,0:T(8,128)(2,1)}, bf16[256,128]{1,0:T(8,128)(2,1)S(1)}, bf16[64,128]{1,0:T(8,128)(2,1)S(1)}, bf16[4,8,32]{2,1,0:T(8,128)(2,1)S(1)}) custom-call(bf16[256,128]{1,0:T(8,128)(2,1)S(1)} %bitcast.12, bf16[16,256]{1,0:T(8,128)(2,1)S(1)} %get-tuple-element.19.vt_ref, bf16[256,256]{1,0:T(8,128)(2,1)S(1)} %get-tuple-element.20.hot_ref), custom_call_target="tpu_custom_call" | custom-call | tf_op jit(solution)/shard_map/gram/pallas_call | solution.py:232
  25.8 14.7 %all-to-all-start.1 = ((bf16[6,32,256]{2,1,0:T(8,128)(2,1)}), bf16[6,32,256]{2,1,0:T(8,128)(2,1)S(1)}, u32[]{:S(2)}, u32[]{:S(2)}) async-start(bf16[6,32,256]{2,1,0:T(8,128)(2,1)} %get-tuple-element.21), calls=%async_computation.1 | async-start | bytes 196608 | tf_op jit(solution)/shard_map/all_to_all | solution.py:247
  40.5 0.0 copy-start
  40.5 0.8 copy-done
  41.2 0.0 copy-start.1
  41.2 3.2 %prep.1 = (f32[4,1024]{1,0:T(4,128)S(1)}, f32[8,128]{1,0:T(8,128)S(1)}, bf16[256,24]{1,0:T(8,128)(2,1)S(1)}, bf16[1024,1024]{1,0:T(8,128)(2,1)S(1)}) custom-call(s32[1]{0:T(128)} %bitcast.8.rank_ref, bf16[4,16,192]{2,1,0:T(8,128)(2,1)S(1)} %copy-done, bf16[16,256]{1,0:T(8,128)(2,1)S(1)} %get-tuple-element.19.vt_ref, ...), custom_call_target="tpu_custom_call" | custom-call | flops 12582912 | bytes 5242880 | tf_op jit(solution)/shard_map/prep/pallas_call | solution.py:232
  44.5 0.9 %all-to-all-done.1.g_ref = bf16[6,32,256]{2,1,0:T(8,128)(2,1)S(1)} async-done(((bf16[6,32,256]{2,1,0:T(8,128)(2,1)}), bf16[6,32,256]{2,1,0:T(8,128)(2,1)S(1)}, u32[]{:S(2)}, u32[]{:S(2)}) %all-to-all-start.1) | async-done | bytes 98336 | tf_op jit(solution)/shard_map/all_to_all | solution.py:247
  45.3 0.0 copy-done.1
  45.3 0.0 copy-start.2
  45.3 4.0 %mlp.1 = (bf16[6,4,2304]{2,1,0:T(4,128)(2,1)S(1)}, f32[4,2048]{1,0:T(4,128)S(1)}, f32[4,128]{1,0:T(4,128)S(1)}) custom-call(bf16[6,32,256]{2,1,0:T(8,128)(2,1)S(1)} %all-to-all-done.1.g_ref, f32[1,2048]{1,0:T(1,128)S(1)} %bitcast.15, f32[4,1024]{1,0:T(4,128)S(1)} %get-tuple-element.23.dh_ref, bf16[1024,1024]{1,0:T(8,128)(2,1)S(1)} %get-tuple-element.24.lo_ref, ...), custom_call_target="tpu_custom_call" | custom-call | tf_op jit(solution)/shard_map/mlp/pallas_call | solution.py:232
  49.3 14.0 %all_to_all.20.c_ref = bf16[6,4,2304]{2,1,0:T(4,128)(2,1)S(1)} all-to-all(bf16[6,4,2304]{2,1,0:T(4,128)(2,1)S(1)} %get-tuple-element.25), channel_id=1, replica_groups={{4,0,2,5,1,3},{10,6,8,11,7,9},{16,12,14,17,13,15},{22,18,20,23,19,21},{..., dimensions={0} | all-to-all | bytes 221184 | tf_op jit(solution)/shard_map/all_to_all | solution.py:247
  63.4 0.9 %grad.1 = (bf16[256,128]{1,0:T(8,128)(2,1)S(1)}, f32[4,256]{1,0:T(4,128)S(1)}) custom-call(bf16[6,4,2304]{2,1,0:T(4,128)(2,1)S(1)} %all_to_all.20.c_ref, f32[1,2048]{1,0:T(1,128)S(1)} %bitcast.16, f32[4,2048]{1,0:T(4,128)S(1)} %get-tuple-element.26.wh_ref, f32[4,128]{1,0:T(4,128)S(1)} %get-tuple-element.27.sc_ref, ...), custom_call_target="tpu_custom_call" | custom-call | tf_op jit(solution)/shard_map/grad/pallas_call | solution.py:232
  64.2 15.6 %all_to_all.21 = bf16[128,2,128]{2,1,0:T(2,128)(2,1)S(1)} all-to-all(bf16[128,2,128]{2,1,0:T(2,128)(2,1)S(1)} %bitcast.14), channel_id=1, replica_groups={{474,480,486,492,498,504,510,516,522,528,534,540,546,552,558,564,570,57..., dimensions={0} | all-to-all | bytes 131072 | tf_op jit(solution)/shard_map/all_to_all | solution.py:247
  79.8 0.0 copy-done.2
  79.8 0.9 %unpool.1 = (bf16[2,32,512]{2,1,0:T(8,128)(2,1)}, bf16[4,16,32]{2,1,0:T(8,128)(2,1)}) custom-call(bf16[256,128]{1,0:T(8,128)(2,1)S(1)} %bitcast.13, s32[2,512]{1,0:T(2,128)S(1)} %bitcast.18, f32[4,256]{1,0:T(4,128)S(1)} %get-tuple-element.32.fm_ref, bf16[4,8,32]{2,1,0:T(8,128)(2,1)S(1)} %get-tuple-element.33.lin_ref), custom_call_target="tpu_custom_call" | custom-call | tf_op jit(solution)/shard_map/unpool/pallas_call | solution.py:232
Async XLA Ops:
  2.5 22.2 %all-to-all-start = ((bf16[128,2,128]{2,1,0:T(2,128)(2,1)}), bf16[128,2,128]{2,1,0:T(2,128)(2,1)S(1)}, u32[]{:S(2)}, u32[]{:S(2)}) async-start(bf16[128,2,128]{2,1,0:T(2,128)(2,1)} %bitcast.22), calls=%async_computation | async-start | bytes 131072 | tf_op jit(solution)/shard_map/all_to_all | solution.py:247
  22.0 0.7 copy-start.3
  22.7 0.7 copy-start.4
  23.3 0.7 copy-start.5
  25.8 19.6 %all-to-all-start.1 = ((bf16[6,32,256]{2,1,0:T(8,128)(2,1)}), bf16[6,32,256]{2,1,0:T(8,128)(2,1)S(1)}, u32[]{:S(2)}, u32[]{:S(2)}) async-start(bf16[6,32,256]{2,1,0:T(8,128)(2,1)} %get-tuple-element.21), calls=%async_computation.1 | async-start | bytes 196608 | tf_op jit(solution)/shard_map/all_to_all | solution.py:247
  40.5 0.8 copy-start
  41.2 4.1 %copy-start.1 = (f32[2048]{0:T(1024)S(1)}, f32[2048]{0:T(1024)}, u32[]{:S(2)}) copy-start(f32[2048]{0:T(1024)} %param.13) | copy-start | bytes 24580
  45.3 34.5 %copy-start.2 = (s32[512,2]{0,1:T(2,128)S(1)}, s32[512,2]{0,1:T(2,128)}, u32[]{:S(2)}) copy-start(s32[512,2]{0,1:T(2,128)} %param.10) | copy-start | bytes 12292

commit v8 on v7

--- a/solution.py
+++ b/solution.py
@@ -15,7 +15,7 @@
 DP = 128
 TURN = 79
 DP_ORDER = [(q + TURN) % DP for q in range(DP)]
-PEERS = [4, 0, 2, 5, 1, 3]
+PEERS = [4, 0, 1, 2, 3, 5]
 H = 1024
 FK = F * K
 ROW = DW * S

time: 81.2 us -> 81.2 us (level)
  no operation moved by 1% of the time
where the time goes in v8:
time: 81.2 us; the launch traced here: 80.7 us
  starting transfers between devices  34.2 us (42%)
  blocking collectives  29.6 us (36%)
  Pallas kernels  12.1 us (15%)
  local copies, waits for them, and re-layouts  2.81 us (3%)
  waiting for transfers between devices  1.3 us (2%)
    all_to_all x2, starting transfers between devices, exchange(): lax.all_to_all(x, axis, split_axis=0, concat_axis=0, axis_index_groups=[o...  34.2 us
    all_to_all x2, blocking collectives, exchange(): lax.all_to_all(x, axis, split_axis=0, concat_axis=0, axis_index_groups=[o...  29.6 us
    pallas_call x7, Pallas kernels, call(): pl.pallas_call(kernel, out_shape=shapes if many else shapes[0], in_specs=...  12.1 us
    unnamed x12, local copies, waits for them, and re-layouts  2.81 us
  transfers between devices with their start and end apart: 2, of which 2 were waited for; matrix products, arithmetic and copies ran while one was open for 0% of the time, Pallas kernels for 4%

profile of v8, /device:TPU:1, one launch (start us, length us, event | category | flops | bytes accessed | tf_op | source)
XLA Modules:
  0.0 80.7 jit_solution(1852970052726827702)
XLA Ops:
  0.6 1.8 %pool.1 = bf16[256,128]{1,0:T(8,128)(2,1)} custom-call(bf16[2,32,512]{2,1,0:T(8,128)(2,1)} %bitcast.23, s32[2,512]{1,0:T(2,128)} %bitcast.17), custom_call_target="tpu_custom_call" | custom-call | tf_op jit(solution)/shard_map/pool/pallas_call | solution.py:232
  2.5 19.5 %all-to-all-start = ((bf16[128,2,128]{2,1,0:T(2,128)(2,1)}), bf16[128,2,128]{2,1,0:T(2,128)(2,1)S(1)}, u32[]{:S(2)}, u32[]{:S(2)}) async-start(bf16[128,2,128]{2,1,0:T(2,128)(2,1)} %bitcast.22), calls=%async_computation | async-start | bytes 131072 | tf_op jit(solution)/shard_map/all_to_all | solution.py:247
  22.0 0.0 copy-start.3
  22.0 0.7 copy-done.3
  22.7 0.0 copy-start.4
  22.7 0.7 copy-done.4
  23.3 0.0 copy-start.5
  23.4 0.7 copy-done.5
  24.0 0.2 slots.1
  24.2 0.4 all-to-all-done
  24.6 1.1 %gram.1 = (bf16[6,32,256]{2,1,0:T(8,128)(2,1)}, bf16[256,128]{1,0:T(8,128)(2,1)S(1)}, bf16[64,128]{1,0:T(8,128)(2,1)S(1)}, bf16[4,8,32]{2,1,0:T(8,128)(2,1)S(1)}) custom-call(bf16[256,128]{1,0:T(8,128)(2,1)S(1)} %bitcast.12, bf16[16,256]{1,0:T(8,128)(2,1)S(1)} %get-tuple-element.19.vt_ref, bf16[256,256]{1,0:T(8,128)(2,1)S(1)} %get-tuple-element.20.hot_ref), custom_call_target="tpu_custom_call" | custom-call | tf_op jit(solution)/shard_map/gram/pallas_call | solution.py:232
  25.8 14.7 %all-to-all-start.1 = ((bf16[6,32,256]{2,1,0:T(8,128)(2,1)}), bf16[6,32,256]{2,1,0:T(8,128)(2,1)S(1)}, u32[]{:S(2)}, u32[]{:S(2)}) async-start(bf16[6,32,256]{2,1,0:T(8,128)(2,1)} %get-tuple-element.21), calls=%async_computation.1 | async-start | bytes 196608 | tf_op jit(solution)/shard_map/all_to_all | solution.py:247
  40.5 0.0 copy-start
  40.5 0.8 copy-done
  41.2 0.0 copy-start.1
  41.2 3.2 %prep.1 = (f32[4,1024]{1,0:T(4,128)S(1)}, f32[8,128]{1,0:T(8,128)S(1)}, bf16[256,24]{1,0:T(8,128)(2,1)S(1)}, bf16[1024,1024]{1,0:T(8,128)(2,1)S(1)}) custom-call(s32[1]{0:T(128)} %bitcast.8.rank_ref, bf16[4,16,192]{2,1,0:T(8,128)(2,1)S(1)} %copy-done, bf16[16,256]{1,0:T(8,128)(2,1)S(1)} %get-tuple-element.19.vt_ref, ...), custom_call_target="tpu_custom_call" | custom-call | flops 12582912 | bytes 5242880 | tf_op jit(solution)/shard_map/prep/pallas_call | solution.py:232
  44.5 0.9 %all-to-all-done.1.g_ref = bf16[6,32,256]{2,1,0:T(8,128)(2,1)S(1)} async-done(((bf16[6,32,256]{2,1,0:T(8,128)(2,1)}), bf16[6,32,256]{2,1,0:T(8,128)(2,1)S(1)}, u32[]{:S(2)}, u32[]{:S(2)}) %all-to-all-start.1) | async-done | bytes 98336 | tf_op jit(solution)/shard_map/all_to_all | solution.py:247
  45.3 0.0 copy-done.1
  45.3 0.0 copy-start.2
  45.3 4.0 %mlp.1 = (bf16[6,4,2304]{2,1,0:T(4,128)(2,1)S(1)}, f32[4,2048]{1,0:T(4,128)S(1)}, f32[4,128]{1,0:T(4,128)S(1)}) custom-call(bf16[6,32,256]{2,1,0:T(8,128)(2,1)S(1)} %all-to-all-done.1.g_ref, f32[1,2048]{1,0:T(1,128)S(1)} %bitcast.15, f32[4,1024]{1,0:T(4,128)S(1)} %get-tuple-element.23.dh_ref, bf16[1024,1024]{1,0:T(8,128)(2,1)S(1)} %get-tuple-element.24.lo_ref, ...), custom_call_target="tpu_custom_call" | custom-call | tf_op jit(solution)/shard_map/mlp/pallas_call | solution.py:232
  49.3 14.0 %all_to_all.20.c_ref = bf16[6,4,2304]{2,1,0:T(4,128)(2,1)S(1)} all-to-all(bf16[6,4,2304]{2,1,0:T(4,128)(2,1)S(1)} %get-tuple-element.25), channel_id=1, replica_groups={{4,0,1,2,3,5},{10,6,7,8,9,11},{16,12,13,14,15,17},{22,18,19,20,21,23},{..., dimensions={0} | all-to-all | bytes 221184 | tf_op jit(solution)/shard_map/all_to_all | solution.py:247
  63.4 0.9 %grad.1 = (bf16[256,128]{1,0:T(8,128)(2,1)S(1)}, f32[4,256]{1,0:T(4,128)S(1)}) custom-call(bf16[6,4,2304]{2,1,0:T(4,128)(2,1)S(1)} %all_to_all.20.c_ref, f32[1,2048]{1,0:T(1,128)S(1)} %bitcast.16, f32[4,2048]{1,0:T(4,128)S(1)} %get-tuple-element.26.wh_ref, f32[4,128]{1,0:T(4,128)S(1)} %get-tuple-element.27.sc_ref, ...), custom_call_target="tpu_custom_call" | custom-call | tf_op jit(solution)/shard_map/grad/pallas_call | solution.py:232
  64.2 15.6 %all_to_all.21 = bf16[128,2,128]{2,1,0:T(2,128)(2,1)S(1)} all-to-all(bf16[128,2,128]{2,1,0:T(2,128)(2,1)S(1)} %bitcast.14), channel_id=1, replica_groups={{474,480,486,492,498,504,510,516,522,528,534,540,546,552,558,564,570,57..., dimensions={0} | all-to-all | bytes 131072 | tf_op jit(solution)/shard_map/all_to_all | solution.py:247
  79.8 0.0 copy-done.2
  79.8 0.9 %unpool.1 = (bf16[2,32,512]{2,1,0:T(8,128)(2,1)}, bf16[4,16,32]{2,1,0:T(8,128)(2,1)}) custom-call(bf16[256,128]{1,0:T(8,128)(2,1)S(1)} %bitcast.13, s32[2,512]{1,0:T(2,128)S(1)} %bitcast.18, f32[4,256]{1,0:T(4,128)S(1)} %get-tuple-element.32.fm_ref, bf16[4,8,32]{2,1,0:T(8,128)(2,1)S(1)} %get-tuple-element.33.lin_ref), custom_call_target="tpu_custom_call" | custom-call | tf_op jit(solution)/shard_map/unpool/pallas_call | solution.py:232
Async XLA Ops:
  2.5 22.2 %all-to-all-start = ((bf16[128,2,128]{2,1,0:T(2,128)(2,1)}), bf16[128,2,128]{2,1,0:T(2,128)(2,1)S(1)}, u32[]{:S(2)}, u32[]{:S(2)}) async-start(bf16[128,2,128]{2,1,0:T(2,128)(2,1)} %bitcast.22), calls=%async_computation | async-start | bytes 131072 | tf_op jit(solution)/shard_map/all_to_all | solution.py:247
  22.0 0.7 copy-start.3
  22.7 0.7 copy-start.4
  23.3 0.7 copy-start.5
  25.8 19.6 %all-to-all-start.1 = ((bf16[6,32,256]{2,1,0:T(8,128)(2,1)}), bf16[6,32,256]{2,1,0:T(8,128)(2,1)S(1)}, u32[]{:S(2)}, u32[]{:S(2)}) async-start(bf16[6,32,256]{2,1,0:T(8,128)(2,1)} %get-tuple-element.21), calls=%async_computation.1 | async-start | bytes 196608 | tf_op jit(solution)/shard_map/all_to_all | solution.py:247
  40.5 0.8 copy-start
  41.2 4.1 %copy-start.1 = (f32[2048]{0:T(1024)S(1)}, f32[2048]{0:T(1024)}, u32[]{:S(2)}) copy-start(f32[2048]{0:T(1024)} %param.13) | copy-start | bytes 24580
  45.3 34.5 %copy-start.2 = (s32[512,2]{0,1:T(2,128)S(1)}, s32[512,2]{0,1:T(2,128)}, u32[]{:S(2)}) copy-start(s32[512,2]{0,1:T(2,128)} %param.10) | copy-start | bytes 12292

commit v9 on v8

--- a/solution.py
+++ b/solution.py
@@ -15,6 +15,7 @@
 DP = 128
 TURN = 79
 DP_ORDER = [(q + TURN) % DP for q in range(DP)]
+PEERS_GRAD = [5, 0, 1, 2, 3, 4]
 PEERS = [4, 0, 1, 2, 3, 5]
 H = 1024
 FK = F * K
@@ -169,7 +170,7 @@
     ow_copy.wait()
     fm = dot(hidden, ow_ref[...])
     for q in range(TP):
-        t = PEERS[q]
+        t = PEERS_GRAD[q]
         c_ref[q, :, :CUT] = d_lo
         c_ref[q, :, CUT:FK] = d_hi
         c_ref[q, :, FK:] = lanes(
@@ -313,7 +314,7 @@
         [pltpu.VMEM((FK - CUT, H), bf16), pltpu.VMEM((H, NF * D), bf16), dma((2,))],
         limit=LARGE,
     )
-    c6 = exchange(c6, "tensor", PEERS)
+    c6 = exchange(c6, "tensor", PEERS_GRAD)
     z, fm = call(
         "grad",
         grad_kernel,

time: 81.2 us -> 81.1 us (level)
  no operation moved by 1% of the time
where the time goes in v9:
time: 81.1 us; the launch traced here: 80.6 us
  starting transfers between devices  34.2 us (42%)
  blocking collectives  29.5 us (36%)
  Pallas kernels  12.1 us (15%)
  local copies, waits for them, and re-layouts  2.81 us (3%)
  waiting for transfers between devices  1.3 us (2%)
    all_to_all x2, starting transfers between devices, exchange(): lax.all_to_all(x, axis, split_axis=0, concat_axis=0, axis_index_groups=[o...  34.2 us
    all_to_all x2, blocking collectives, exchange(): lax.all_to_all(x, axis, split_axis=0, concat_axis=0, axis_index_groups=[o...  29.5 us
    pallas_call x7, Pallas kernels, call(): pl.pallas_call(kernel, out_shape=shapes if many else shapes[0], in_specs=...  12.1 us
    unnamed x12, local copies, waits for them, and re-layouts  2.81 us
  transfers between devices with their start and end apart: 2, of which 2 were waited for; matrix products, arithmetic and copies ran while one was open for 0% of the time, Pallas kernels for 4%

profile of v9, /device:TPU:1, one launch (start us, length us, event | category | flops | bytes accessed | tf_op | source)
XLA Modules:
  0.0 80.6 jit_solution(2813132752983771798)
XLA Ops:
  0.6 1.8 %pool.1 = bf16[256,128]{1,0:T(8,128)(2,1)} custom-call(bf16[2,32,512]{2,1,0:T(8,128)(2,1)} %bitcast.23, s32[2,512]{1,0:T(2,128)} %bitcast.17), custom_call_target="tpu_custom_call" | custom-call | tf_op jit(solution)/shard_map/pool/pallas_call | solution.py:233
  2.5 19.5 %all-to-all-start = ((bf16[128,2,128]{2,1,0:T(2,128)(2,1)}), bf16[128,2,128]{2,1,0:T(2,128)(2,1)S(1)}, u32[]{:S(2)}, u32[]{:S(2)}) async-start(bf16[128,2,128]{2,1,0:T(2,128)(2,1)} %bitcast.22), calls=%async_computation | async-start | bytes 131072 | tf_op jit(solution)/shard_map/all_to_all | solution.py:248
  22.0 0.0 copy-start.3
  22.0 0.7 copy-done.3
  22.7 0.0 copy-start.4
  22.7 0.7 copy-done.4
  23.3 0.0 copy-start.5
  23.4 0.7 copy-done.5
  24.0 0.2 slots.1
  24.2 0.4 all-to-all-done
  24.6 1.1 %gram.1 = (bf16[6,32,256]{2,1,0:T(8,128)(2,1)}, bf16[256,128]{1,0:T(8,128)(2,1)S(1)}, bf16[64,128]{1,0:T(8,128)(2,1)S(1)}, bf16[4,8,32]{2,1,0:T(8,128)(2,1)S(1)}) custom-call(bf16[256,128]{1,0:T(8,128)(2,1)S(1)} %bitcast.12, bf16[16,256]{1,0:T(8,128)(2,1)S(1)} %get-tuple-element.19.vt_ref, bf16[256,256]{1,0:T(8,128)(2,1)S(1)} %get-tuple-element.20.hot_ref), custom_call_target="tpu_custom_call" | custom-call | tf_op jit(solution)/shard_map/gram/pallas_call | solution.py:233
  25.8 14.7 %all-to-all-start.1 = ((bf16[6,32,256]{2,1,0:T(8,128)(2,1)}), bf16[6,32,256]{2,1,0:T(8,128)(2,1)S(1)}, u32[]{:S(2)}, u32[]{:S(2)}) async-start(bf16[6,32,256]{2,1,0:T(8,128)(2,1)} %get-tuple-element.21), calls=%async_computation.1 | async-start | bytes 196608 | tf_op jit(solution)/shard_map/all_to_all | solution.py:248
  40.5 0.0 copy-start
  40.5 0.8 copy-done
  41.2 0.0 copy-start.1
  41.2 3.2 %prep.1 = (f32[4,1024]{1,0:T(4,128)S(1)}, f32[8,128]{1,0:T(8,128)S(1)}, bf16[256,24]{1,0:T(8,128)(2,1)S(1)}, bf16[1024,1024]{1,0:T(8,128)(2,1)S(1)}) custom-call(s32[1]{0:T(128)} %bitcast.8.rank_ref, bf16[4,16,192]{2,1,0:T(8,128)(2,1)S(1)} %copy-done, bf16[16,256]{1,0:T(8,128)(2,1)S(1)} %get-tuple-element.19.vt_ref, ...), custom_call_target="tpu_custom_call" | custom-call | flops 12582912 | bytes 5242880 | tf_op jit(solution)/shard_map/prep/pallas_call | solution.py:233
  44.5 0.9 %all-to-all-done.1.g_ref = bf16[6,32,256]{2,1,0:T(8,128)(2,1)S(1)} async-done(((bf16[6,32,256]{2,1,0:T(8,128)(2,1)}), bf16[6,32,256]{2,1,0:T(8,128)(2,1)S(1)}, u32[]{:S(2)}, u32[]{:S(2)}) %all-to-all-start.1) | async-done | bytes 98336 | tf_op jit(solution)/shard_map/all_to_all | solution.py:248
  45.3 0.0 copy-done.1
  45.3 0.0 copy-start.2
  45.3 4.0 %mlp.1 = (bf16[6,4,2304]{2,1,0:T(4,128)(2,1)S(1)}, f32[4,2048]{1,0:T(4,128)S(1)}, f32[4,128]{1,0:T(4,128)S(1)}) custom-call(bf16[6,32,256]{2,1,0:T(8,128)(2,1)S(1)} %all-to-all-done.1.g_ref, f32[1,2048]{1,0:T(1,128)S(1)} %bitcast.15, f32[4,1024]{1,0:T(4,128)S(1)} %get-tuple-element.23.dh_ref, bf16[1024,1024]{1,0:T(8,128)(2,1)S(1)} %get-tuple-element.24.lo_ref, ...), custom_call_target="tpu_custom_call" | custom-call | tf_op jit(solution)/shard_map/mlp/pallas_call | solution.py:233
  49.3 14.0 %all_to_all.20.c_ref = bf16[6,4,2304]{2,1,0:T(4,128)(2,1)S(1)} all-to-all(bf16[6,4,2304]{2,1,0:T(4,128)(2,1)S(1)} %get-tuple-element.25), channel_id=1, replica_groups={{5,0,1,2,3,4},{11,6,7,8,9,10},{17,12,13,14,15,16},{23,18,19,20,21,22},{..., dimensions={0} | all-to-all | bytes 221184 | tf_op jit(solution)/shard_map/all_to_all | solution.py:248
  63.3 0.9 %grad.1 = (bf16[256,128]{1,0:T(8,128)(2,1)S(1)}, f32[4,256]{1,0:T(4,128)S(1)}) custom-call(bf16[6,4,2304]{2,1,0:T(4,128)(2,1)S(1)} %all_to_all.20.c_ref, f32[1,2048]{1,0:T(1,128)S(1)} %bitcast.16, f32[4,2048]{1,0:T(4,128)S(1)} %get-tuple-element.26.wh_ref, f32[4,128]{1,0:T(4,128)S(1)} %get-tuple-element.27.sc_ref, ...), custom_call_target="tpu_custom_call" | custom-call | tf_op jit(solution)/shard_map/grad/pallas_call | solution.py:233
  64.1 15.6 %all_to_all.21 = bf16[128,2,128]{2,1,0:T(2,128)(2,1)S(1)} all-to-all(bf16[128,2,128]{2,1,0:T(2,128)(2,1)S(1)} %bitcast.14), channel_id=1, replica_groups={{474,480,486,492,498,504,510,516,522,528,534,540,546,552,558,564,570,57..., dimensions={0} | all-to-all | bytes 131072 | tf_op jit(solution)/shard_map/all_to_all | solution.py:248
  79.7 0.0 copy-done.2
  79.7 0.9 %unpool.1 = (bf16[2,32,512]{2,1,0:T(8,128)(2,1)}, bf16[4,16,32]{2,1,0:T(8,128)(2,1)}) custom-call(bf16[256,128]{1,0:T(8,128)(2,1)S(1)} %bitcast.13, s32[2,512]{1,0:T(2,128)S(1)} %bitcast.18, f32[4,256]{1,0:T(4,128)S(1)} %get-tuple-element.32.fm_ref, bf16[4,8,32]{2,1,0:T(8,128)(2,1)S(1)} %get-tuple-element.33.lin_ref), custom_call_target="tpu_custom_call" | custom-call | tf_op jit(solution)/shard_map/unpool/pallas_call | solution.py:233
Async XLA Ops:
  2.5 22.2 %all-to-all-start = ((bf16[128,2,128]{2,1,0:T(2,128)(2,1)}), bf16[128,2,128]{2,1,0:T(2,128)(2,1)S(1)}, u32[]{:S(2)}, u32[]{:S(2)}) async-start(bf16[128,2,128]{2,1,0:T(2,128)(2,1)} %bitcast.22), calls=%async_computation | async-start | bytes 131072 | tf_op jit(solution)/shard_map/all_to_all | solution.py:248
  22.0 0.7 copy-start.3
  22.7 0.7 copy-start.4
  23.3 0.7 copy-start.5
  25.8 19.6 %all-to-all-start.1 = ((bf16[6,32,256]{2,1,0:T(8,128)(2,1)}), bf16[6,32,256]{2,1,0:T(8,128)(2,1)S(1)}, u32[]{:S(2)}, u32[]{:S(2)}) async-start(bf16[6,32,256]{2,1,0:T(8,128)(2,1)} %get-tuple-element.21), calls=%async_computation.1 | async-start | bytes 196608 | tf_op jit(solution)/shard_map/all_to_all | solution.py:248
  40.5 0.8 copy-start
  41.2 4.1 %copy-start.1 = (f32[2048]{0:T(1024)S(1)}, f32[2048]{0:T(1024)}, u32[]{:S(2)}) copy-start(f32[2048]{0:T(1024)} %param.13) | copy-start | bytes 24580
  45.3 34.4 %copy-start.2 = (s32[512,2]{0,1:T(2,128)S(1)}, s32[512,2]{0,1:T(2,128)}, u32[]{:S(2)}) copy-start(s32[512,2]{0,1:T(2,128)} %param.10) | copy-start | bytes 12292
